TPU v7x, 32 devices: a whole 2x2x4 slice. The times are simulated.
32 devices in a mesh: mem: 2 (over x), lat: 2 (over y), lon: 8 (over z, core).
Axes of the slice: x: 2, y: 2, z: 4, core: 2. Of those that a mesh axis runs over, the one named last changes fastest.
Arguments:
- members: float32 [2, 87, 16, 1024], P('mem', None, 'lat', 'lon'), may hold values from -6 to 6
- target: float32 [87, 16, 1024], P(None, 'lat', 'lon'), may hold values from -6 to 6
Outputs:
- gradient: float32 [2, 87, 16, 1024], P('mem', None, 'lat', 'lon')
- loss: float32 [], replicated
All inputs are finite; a program needn't handle non-finite values.
Results may differ from a plain program's by a relative error of at most 0.0001.
Values sent between devices are 32-bit elements; how exact they have to be, the bound alone decides.
A program may use at most 64 MiB of HBM per device.

v0:
```python
import jax
import jax.numpy as jnp
from jax import lax
from jax.sharding import PartitionSpec as P

LEVELS = 7


smooth_eps = 0.05


def passed_along(value, axis, by):
    count = lax.axis_size(axis)
    pairs = [(i, i + by) for i in range(count) if 0 <= i + by < count]
    return lax.ppermute(value, axis, pairs)


def from_behind(value, axis, steps):
    count = lax.axis_size(axis)
    pairs = [(source, (source + steps) % count) for source in range(count)]
    return lax.ppermute(value, axis, pairs)


def from_partner(value, axis, stride):
    mask = 2**stride
    pairs = [(source, source ^ mask) for source in range(lax.axis_size(axis))]
    return lax.ppermute(value, axis, pairs)


def soft_abs(values):
    return jnp.sqrt(values * values + smooth_eps * smooth_eps)


def lat_weights(row_count):
    row_index = jnp.arange(row_count, dtype=jnp.float32)
    return jnp.cos((89.875 - 0.25 * row_index) * (jnp.pi / 180.0))


def rows_ahead(values, reach):
    row_count = values.shape[-2]
    axis_count = lax.axis_size("lat")
    hops, remain = divmod(reach, row_count)
    portions = []
    for distance, portion in ((hops, values[..., remain:, :]), (hops + 1, values[..., :remain, :])):
        if portion.shape[-2] == 0:
            continue
        if distance == 0:
            portions.append(portion)
        elif distance >= axis_count:
            portions.append(jnp.zeros_like(portion))
        else:
            portions.append(passed_along(portion, "lat", -distance))
    return jnp.concatenate(portions, axis=-2)


def cols_ahead(values, reach):
    col_count = values.shape[-1]
    axis_count = lax.axis_size("lon")
    hops, remain = divmod(reach, col_count)
    portions = []
    for distance, portion in ((hops, values[..., remain:]), (hops + 1, values[..., :remain])):
        if distance % axis_count == 0:
            portions.append(portion)
        else:
            portions.append(from_behind(portion, "lon", -(distance % axis_count)))
    return jnp.concatenate(portions, axis=-1)


def rows_behind(values, reach):
    row_count = values.shape[-2]
    axis_count = lax.axis_size("lat")
    hops, remain = divmod(reach, row_count)
    portions = []
    for distance, portion in (
        (hops + 1, values[..., row_count - remain :, :]),
        (hops, values[..., : row_count - remain, :]),
    ):
        if portion.shape[-2] == 0:
            continue
        if distance == 0:
            portions.append(portion)
        elif distance >= axis_count:
            portions.append(jnp.zeros_like(portion))
        else:
            portions.append(passed_along(portion, "lat", distance))
    return jnp.concatenate(portions, axis=-2)


def cols_behind(values, reach):
    col_count = values.shape[-1]
    axis_count = lax.axis_size("lon")
    hops, remain = divmod(reach, col_count)
    portions = []
    for distance, portion in (
        (hops + 1, values[..., col_count - remain :]),
        (hops, values[..., : col_count - remain]),
    ):
        if distance % axis_count == 0:
            portions.append(portion)
        else:
            portions.append(from_behind(portion, "lon", distance % axis_count))
    return jnp.concatenate(portions, axis=-1)


def shards(members, target):
    own_field = members[0]
    channels, row_count, col_count = own_field.shape
    nlat_total = row_count * lax.axis_size("lat")
    nlon_total = col_count * lax.axis_size("lon")
    row_start = lax.axis_index("lat") * row_count
    current = lat_weights(nlat_total)
    global_boxes = [current]
    for level in range(LEVELS):
        reach = 2**level
        current = current + jnp.pad(current, (0, reach))[reach : reach + nlat_total]
        global_boxes.append(current)
    own_boxes = [lax.dynamic_slice_in_dim(vector, row_start, row_count) for vector in global_boxes]
    box_totals = [jnp.sum(vector) for vector in global_boxes]
    own_weight = own_boxes[0][:, None]
    weighted = own_weight * (own_field - target)
    box_sum = weighted[None]
    loss_local = jnp.zeros((), jnp.float32)
    cotangents = []
    for scale in range(LEVELS + 1):
        if scale > 0:
            reach = 2 ** (scale - 1)
            box_sum = box_sum + rows_ahead(box_sum, reach)
            box_sum = box_sum + cols_ahead(box_sum, reach)
        lat_box = own_boxes[scale]
        pool_cells = 2.0**scale
        pooled = box_sum / (pool_cells * lat_box)[:, None]
        own_pool = pooled[0]
        partner_pool = from_partner(own_pool, "mem", 0)
        spread = own_pool - partner_pool
        spread_abs = soft_abs(spread)
        own_abs = soft_abs(own_pool)
        score = 0.5 * (own_abs + soft_abs(partner_pool)) - 0.5 * spread_abs
        loss_local = loss_local + jnp.sum(lat_box[:, None] * score) / (
            channels * nlon_total * box_totals[scale]
        )
        factor = 0.5 * nlat_total / (box_totals[scale] * pool_cells)
        cotangents.append((own_pool / own_abs - spread / spread_abs) * factor)
    loss = lax.psum(loss_local, ("lat", "lon"))
    adjoint = cotangents[LEVELS]
    for level in reversed(range(LEVELS)):
        reach = 2**level
        adjoint = adjoint + cols_behind(adjoint, reach)
        adjoint = adjoint + rows_behind(adjoint, reach)
        adjoint = adjoint + cotangents[level]
    gradient = (own_weight * adjoint)[None]
    return (gradient, loss)


def solution(mesh):
    placed = (P("mem", None, "lat", "lon"), P(None, "lat", "lon"))
    return jax.shard_map(
        shards,
        mesh=mesh,
        in_specs=placed,
        out_specs=(P("mem", None, "lat", "lon"), P()),
        check_vma=False,
    )
```

profile of v0, /device:TPU:0, one launch (start us, length us, event | category | flops | bytes accessed | tf_op | source)
XLA Modules:
  0.0 246.3 jit_solution(17978471200319992570)
XLA Ops:
  12.3 4.7 %collective-permute-done.1 = f32[1,87,8,1]{3,2,1,0:T(8,128)S(1)} collective-permute-done((f32[1,87,8,1]{3,2,1,0:T(8,128)S(1)}, f32[1,87,8,1]{3,2,1,0:T(8,128)S(1)}, u32[]{:S(2)}, u32[]{:S(2)}) %collective-permute-start.1) | collective-permute-done | bytes 2816 | tf_op jit(solution)/shard_map/ppermute | solution.py:21
  19.8 5.1 %collective-permute-done.2 = f32[1,87,2,128]{3,2,1,0:T(2,128)S(1)} collective-permute-done((f32[1,87,2,128]{3,2,1,0:T(2,128)S(1)}, f32[1,87,2,128]{3,2,1,0:T(2,128)S(1)}, u32[]{:S(2)}, u32[]{:S(2)}) %collective-permute-start.2) | collective-permute-done | bytes 89120 | tf_op jit(solution)/shard_map/ppermute | solution.py:15
  27.7 4.7 %collective-permute-done.3 = f32[1,87,8,2]{3,2,1,0:T(8,128)S(1)} collective-permute-done((f32[1,87,8,2]{3,2,1,0:T(8,128)S(1)}, f32[1,87,8,2]{3,2,1,0:T(8,128)S(1)}, u32[]{:S(2)}, u32[]{:S(2)}) %collective-permute-start.3) | collective-permute-done | bytes 5600 | tf_op jit(solution)/shard_map/ppermute | solution.py:21
  35.6 5.3 %collective-permute-done.4 = f32[1,87,4,128]{3,2,1,0:T(4,128)S(1)} collective-permute-done((f32[1,87,4,128]{3,2,1,0:T(4,128)S(1)}, f32[1,87,4,128]{3,2,1,0:T(4,128)S(1)}, u32[]{:S(2)}, u32[]{:S(2)}) %collective-permute-start.4) | collective-permute-done | bytes 178208 | tf_op jit(solution)/shard_map/ppermute | solution.py:15
  43.7 4.7 %collective-permute-done.5 = f32[1,87,8,4]{3,2,1,0:T(8,128)S(1)} collective-permute-done((f32[1,87,8,4]{3,2,1,0:T(8,128)S(1)}, f32[1,87,8,4]{3,2,1,0:T(8,128)S(1)}, u32[]{:S(2)}, u32[]{:S(2)}) %collective-permute-start.5) | collective-permute-done | bytes 11168 | tf_op jit(solution)/shard_map/ppermute | solution.py:21
  51.4 7.3 %collective-permute-done.6 = f32[1,87,8,128]{3,2,1,0:T(8,128)S(1)} collective-permute-done((f32[1,87,8,128]{3,2,1,0:T(8,128)S(1)}, f32[1,87,8,128]{3,2,1,0:T(8,128)S(1)}, u32[]{:S(2)}, u32[]{:S(2)}) %collective-permute-start.6) | collective-permute-done | bytes 356384 | tf_op jit(solution)/shard_map/ppermute | solution.py:15
  61.5 4.7 %collective-permute-done.7 = f32[1,87,8,8]{3,2,1,0:T(8,128)S(1)} collective-permute-done((f32[1,87,8,8]{3,2,1,0:T(8,128)S(1)}, f32[1,87,8,8]{3,2,1,0:T(8,128)S(1)}, u32[]{:S(2)}, u32[]{:S(2)}) %collective-permute-start.7) | collective-permute-done | bytes 22304 | tf_op jit(solution)/shard_map/ppermute | solution.py:21
  71.0 4.7 %collective-permute-done.8 = f32[1,87,8,16]{3,2,1,0:T(8,128)S(1)} collective-permute-done((f32[1,87,8,16]{3,2,1,0:T(8,128)S(1)}, f32[1,87,8,16]{3,2,1,0:T(8,128)S(1)}, u32[]{:S(2)}, u32[]{:S(2)}) %collective-permute-start.8) | collective-permute-done | bytes 44576 | tf_op jit(solution)/shard_map/ppermute | solution.py:21
  79.8 4.7 %collective-permute-done.9 = f32[1,87,8,32]{3,2,1,0:T(8,128)S(1)} collective-permute-done((f32[1,87,8,32]{3,2,1,0:T(8,128)S(1)}, f32[1,87,8,32]{3,2,1,0:T(8,128)S(1)}, u32[]{:S(2)}, u32[]{:S(2)}) %collective-permute-start.9) | collective-permute-done | bytes 89120 | tf_op jit(solution)/shard_map/ppermute | solution.py:21
  88.7 4.9 %collective-permute-done.10 = f32[1,87,8,64]{3,2,1,0:T(8,128)S(1)} collective-permute-done((f32[1,87,8,64]{3,2,1,0:T(8,128)S(1)}, f32[1,87,8,64]{3,2,1,0:T(8,128)S(1)}, u32[]{:S(2)}, u32[]{:S(2)}) %collective-permute-start.10) | collective-permute-done | bytes 178208 | tf_op jit(solution)/shard_map/ppermute | solution.py:21
  96.5 6.5 %collective-permute-done.11 = f32[87,8,128]{2,1,0:T(8,128)} collective-permute-done((f32[87,8,128]{2,1,0:T(8,128)S(1)}, f32[87,8,128]{2,1,0:T(8,128)}, u32[]{:S(2)}, u32[]{:S(2)}) %collective-permute-start.11) | collective-permute-done | bytes 356384 | tf_op jit(solution)/shard_map/ppermute | solution.py:27
  108.8 5.4 %collective-permute-done.12 = f32[87,8,64]{2,1,0:T(8,128)} collective-permute-done((f32[87,8,64]{2,1,0:T(8,128)}, f32[87,8,64]{2,1,0:T(8,128)}, u32[]{:S(2)}, u32[]{:S(2)}) %collective-permute-start.12) | collective-permute-done | bytes 178208 | tf_op jit(solution)/shard_map/ppermute | solution.py:21
  118.3 6.5 %collective-permute-done.14 = f32[87,8,32]{2,1,0:T(8,128)} collective-permute-done((f32[87,8,32]{2,1,0:T(8,128)S(1)}, f32[87,8,32]{2,1,0:T(8,128)}, u32[]{:S(2)}, u32[]{:S(2)}) %collective-permute-start.14) | collective-permute-done | bytes 89120 | tf_op jit(solution)/shard_map/ppermute | solution.py:21
  127.8 8.3 %collective-permute-done.16 = f32[87,8,16]{2,1,0:T(8,128)} collective-permute-done((f32[87,8,16]{2,1,0:T(8,128)}, f32[87,8,16]{2,1,0:T(8,128)}, u32[]{:S(2)}, u32[]{:S(2)}) %collective-permute-start.16) | collective-permute-done | bytes 44576 | tf_op jit(solution)/shard_map/ppermute | solution.py:21
  136.1 3.9 %multiply_reduce_fusion = (f32[]{:T(128)}, f32[]{:T(128)}, f32[]{:T(128)}, f32[]{:T(128)}, f32[87,8,128]{2,1,0:T(8,128)S(1)}) fusion(f32[87,8,128]{2,1,0:T(8,128)} %collective-permute-done.11, f32[87,8,128]{2,1,0:T(8,128)S(1)} %fusion.1, f32[8]{0:T(128)S(1)} %get-tuple-element.29, f32[87,8,128]{2,1,0:T(8,128)S(1)} %get-tuple-element.30, ...), kind=kLoop, calls=%fused_computation.37 | loop fusion | flops 5256188 | bytes 3919924 | tf_op jit(solution)/shard_map/reduce_sum | solution.py:138
  142.4 6.3 %collective-permute-done.18 = f32[87,8,8]{2,1,0:T(8,128)S(1)} collective-permute-done((f32[87,8,8]{2,1,0:T(8,128)S(1)}, f32[87,8,8]{2,1,0:T(8,128)S(1)}, u32[]{:S(2)}, u32[]{:S(2)}) %collective-permute-start.18) | collective-permute-done | bytes 22304 | tf_op jit(solution)/shard_map/ppermute | solution.py:21
  151.4 4.2 %collective-permute-done.19 = f32[87,8,128]{2,1,0:T(8,128)S(1)} collective-permute-done((f32[87,8,128]{2,1,0:T(8,128)S(1)}, f32[87,8,128]{2,1,0:T(8,128)S(1)}, u32[]{:S(2)}, u32[]{:S(2)}) %collective-permute-start.19) | collective-permute-done | bytes 356384 | tf_op jit(solution)/shard_map/ppermute | solution.py:15
  159.3 6.3 %collective-permute-done.21 = f32[87,8,4]{2,1,0:T(8,128)S(1)} collective-permute-done((f32[87,8,4]{2,1,0:T(8,128)S(1)}, f32[87,8,4]{2,1,0:T(8,128)S(1)}, u32[]{:S(2)}, u32[]{:S(2)}) %collective-permute-start.21) | collective-permute-done | bytes 11168 | tf_op jit(solution)/shard_map/ppermute | solution.py:21
  165.9 4.5 %collective-permute-start.22 = (f32[87,4,128]{2,1,0:T(4,128)S(1)}, f32[87,4,128]{2,1,0:T(4,128)S(1)}, u32[]{:S(2)}, u32[]{:S(2)}) collective-permute-start(f32[87,4,128]{2,1,0:T(4,128)S(1)} %get-tuple-element.45), channel_id=1, source_target_pairs={{0,8},{1,9},{2,10},{3,11},{4,12},{5,13},{6,14},{7,15},{16,24},{17,... | collective-permute-start | bytes 534536 | tf_op jit(solution)/shard_map/ppermute | solution.py:15
  174.9 8.6 %collective-permute-done.24 = f32[87,8,2]{2,1,0:T(8,128)S(1)} collective-permute-done((f32[87,8,2]{2,1,0:T(8,128)S(1)}, f32[87,8,2]{2,1,0:T(8,128)S(1)}, u32[]{:S(2)}, u32[]{:S(2)}) %collective-permute-start.24) | collective-permute-done | bytes 5600 | tf_op jit(solution)/shard_map/ppermute | solution.py:21
  183.7 4.4 %collective-permute-start.25 = (f32[87,2,128]{2,1,0:T(2,128)S(1)}, f32[87,2,128]{2,1,0:T(2,128)S(1)}, u32[]{:S(2)}, u32[]{:S(2)}) collective-permute-start(f32[87,2,128]{2,1,0:T(2,128)S(1)} %slice.213), channel_id=1, source_target_pairs={{0,8},{1,9},{2,10},{3,11},{4,12},{5,13},{6,14},{7,15},{16,24},{17,... | collective-permute-start | bytes 267272 | tf_op jit(solution)/shard_map/ppermute | solution.py:15
  191.8 8.6 %collective-permute-done.27 = f32[87,8,1]{2,1,0:T(8,128)S(1)} collective-permute-done((f32[87,8,1]{2,1,0:T(8,128)S(1)}, f32[87,8,1]{2,1,0:T(8,128)S(1)}, u32[]{:S(2)}, u32[]{:S(2)}) %collective-permute-start.27) | collective-permute-done | bytes 2816 | tf_op jit(solution)/shard_map/ppermute | solution.py:21
  200.6 4.1 %collective-permute-start.28 = (f32[87,1,128]{2,1,0:T(1,128)S(1)}, f32[87,1,128]{2,1,0:T(1,128)S(1)}, u32[]{:S(2)}, u32[]{:S(2)}) collective-permute-start(f32[87,1,128]{2,1,0:T(1,128)S(1)} %slice.217), channel_id=1, source_target_pairs={{0,8},{1,9},{2,10},{3,11},{4,12},{5,13},{6,14},{7,15},{16,24},{17,... | collective-permute-start | bytes 133640 | tf_op jit(solution)/shard_map/ppermute | solution.py:15
  216.3 30.0 %psum.7 = f32[]{:T(128)} all-reduce(f32[]{:T(128)S(6)} %add.335), channel_id=1, replica_groups=mesh['mem'=2,'lat'=2,'lon'=8] {'lat','lon'}, use_global_device_ids=true, to_apply=%region_13.14 | all-reduce | flops 1 | bytes 8 | tf_op jit(solution)/shard_map/psum | solution.py:143
  (109 shorter events, 73.2 us)
Async XLA Ops:
  9.1 8.0 %collective-permute-start.1 = (f32[1,87,8,1]{3,2,1,0:T(8,128)S(1)}, f32[1,87,8,1]{3,2,1,0:T(8,128)S(1)}, u32[]{:S(2)}, u32[]{:S(2)}) collective-permute-start(f32[1,87,8,1]{3,2,1,0:T(8,128)S(1)} %bitcast.75), channel_id=1, source_target_pairs={{0,7},{1,0},{2,1},{3,2},{4,3},{5,4},{6,5},{7,6},{8,15},{9,8},{10,9... | collective-permute-start | bytes 8360 | tf_op jit(solution)/shard_map/ppermute | solution.py:21
  25.0 7.5 %collective-permute-start.3 = (f32[1,87,8,2]{3,2,1,0:T(8,128)S(1)}, f32[1,87,8,2]{3,2,1,0:T(8,128)S(1)}, u32[]{:S(2)}, u32[]{:S(2)}) collective-permute-start(f32[1,87,8,2]{3,2,1,0:T(8,128)S(1)} %bitcast.77), channel_id=1, source_target_pairs={{0,7},{1,0},{2,1},{3,2},{4,3},{5,4},{6,5},{7,6},{8,15},{9,8},{10,9... | collective-permute-start | bytes 16712 | tf_op jit(solution)/shard_map/ppermute | solution.py:21
  40.9 7.5 %collective-permute-start.5 = (f32[1,87,8,4]{3,2,1,0:T(8,128)S(1)}, f32[1,87,8,4]{3,2,1,0:T(8,128)S(1)}, u32[]{:S(2)}, u32[]{:S(2)}) collective-permute-start(f32[1,87,8,4]{3,2,1,0:T(8,128)S(1)} %bitcast.76), channel_id=1, source_target_pairs={{0,7},{1,0},{2,1},{3,2},{4,3},{5,4},{6,5},{7,6},{8,15},{9,8},{10,9... | collective-permute-start | bytes 33416 | tf_op jit(solution)/shard_map/ppermute | solution.py:21
  49.4 9.3 %collective-permute-start.6 = (f32[1,87,8,128]{3,2,1,0:T(8,128)S(1)}, f32[1,87,8,128]{3,2,1,0:T(8,128)S(1)}, u32[]{:S(2)}, u32[]{:S(2)}) collective-permute-start(f32[1,87,8,128]{3,2,1,0:T(8,128)S(1)} %bitcast.71), channel_id=1, source_target_pairs={{8,0},{9,1},{10,2},{11,3},{12,4},{13,5},{14,6},{15,7},{24,16},{25,... | collective-permute-start | bytes 1069064 | tf_op jit(solution)/shard_map/ppermute | solution.py:15
  58.7 7.5 %collective-permute-start.7 = (f32[1,87,8,8]{3,2,1,0:T(8,128)S(1)}, f32[1,87,8,8]{3,2,1,0:T(8,128)S(1)}, u32[]{:S(2)}, u32[]{:S(2)}) collective-permute-start(f32[1,87,8,8]{3,2,1,0:T(8,128)S(1)} %bitcast.72), channel_id=1, source_target_pairs={{0,7},{1,0},{2,1},{3,2},{4,3},{5,4},{6,5},{7,6},{8,15},{9,8},{10,9... | collective-permute-start | bytes 66824 | tf_op jit(solution)/shard_map/ppermute | solution.py:21
  67.1 8.6 %collective-permute-start.8 = (f32[1,87,8,16]{3,2,1,0:T(8,128)S(1)}, f32[1,87,8,16]{3,2,1,0:T(8,128)S(1)}, u32[]{:S(2)}, u32[]{:S(2)}) collective-permute-start(f32[1,87,8,16]{3,2,1,0:T(8,128)S(1)} %bitcast.73), channel_id=1, source_target_pairs={{0,7},{1,0},{2,1},{3,2},{4,3},{5,4},{6,5},{7,6},{8,15},{9,8},{10,9... | collective-permute-start | bytes 133640 | tf_op jit(solution)/shard_map/ppermute | solution.py:21
  75.9 8.7 %collective-permute-start.9 = (f32[1,87,8,32]{3,2,1,0:T(8,128)S(1)}, f32[1,87,8,32]{3,2,1,0:T(8,128)S(1)}, u32[]{:S(2)}, u32[]{:S(2)}) collective-permute-start(f32[1,87,8,32]{3,2,1,0:T(8,128)S(1)} %bitcast.74), channel_id=1, source_target_pairs={{0,7},{1,0},{2,1},{3,2},{4,3},{5,4},{6,5},{7,6},{8,15},{9,8},{10,9... | collective-permute-start | bytes 267272 | tf_op jit(solution)/shard_map/ppermute | solution.py:21
  84.9 8.7 %collective-permute-start.10 = (f32[1,87,8,64]{3,2,1,0:T(8,128)S(1)}, f32[1,87,8,64]{3,2,1,0:T(8,128)S(1)}, u32[]{:S(2)}, u32[]{:S(2)}) collective-permute-start(f32[1,87,8,64]{3,2,1,0:T(8,128)S(1)} %get-tuple-element.50), channel_id=1, source_target_pairs={{0,7},{1,0},{2,1},{3,2},{4,3},{5,4},{6,5},{7,6},{8,15},{9,8},{10,9... | collective-permute-start | bytes 534536 | tf_op jit(solution)/shard_map/ppermute | solution.py:21
  93.7 9.3 %collective-permute-start.11 = (f32[87,8,128]{2,1,0:T(8,128)S(1)}, f32[87,8,128]{2,1,0:T(8,128)}, u32[]{:S(2)}, u32[]{:S(2)}) collective-permute-start(f32[87,8,128]{2,1,0:T(8,128)S(1)} %fusion.1), channel_id=1, source_target_pairs={{0,16},{16,0},{1,17},{17,1},{2,18},{18,2},{3,19},{19,3},{4,20},{20... | collective-permute-start | bytes 1069064 | tf_op jit(solution)/shard_map/ppermute | solution.py:27
  95.9 12.9 %collective-permute-start.13 = (f32[87,8,128]{2,1,0:T(8,128)S(1)}, f32[87,8,128]{2,1,0:T(8,128)S(1)}, u32[]{:S(2)}, u32[]{:S(2)}) collective-permute-start(f32[87,8,128]{2,1,0:T(8,128)S(1)} %get-tuple-element.32), channel_id=1, source_target_pairs={{0,16},{16,0},{1,17},{17,1},{2,18},{18,2},{3,19},{19,3},{4,20},{20... | collective-permute-start | bytes 1069064 | tf_op jit(solution)/shard_map/ppermute | solution.py:27
  105.3 8.9 %collective-permute-start.12 = (f32[87,8,64]{2,1,0:T(8,128)}, f32[87,8,64]{2,1,0:T(8,128)}, u32[]{:S(2)}, u32[]{:S(2)}) collective-permute-start(f32[87,8,64]{2,1,0:T(8,128)} %get-tuple-element.47), channel_id=1, source_target_pairs={{0,1},{1,2},{2,3},{3,4},{4,5},{5,6},{6,7},{7,0},{8,9},{9,10},{10,1... | collective-permute-start | bytes 534536 | tf_op jit(solution)/shard_map/ppermute | solution.py:21
  105.3 13.0 %collective-permute-start.15 = (f32[87,8,128]{2,1,0:T(8,128)S(1)}, f32[87,8,128]{2,1,0:T(8,128)}, u32[]{:S(2)}, u32[]{:S(2)}) collective-permute-start(f32[87,8,128]{2,1,0:T(8,128)S(1)} %get-tuple-element.30), channel_id=1, source_target_pairs={{0,16},{16,0},{1,17},{17,1},{2,18},{18,2},{3,19},{19,3},{4,20},{20... | collective-permute-start | bytes 1069064 | tf_op jit(solution)/shard_map/ppermute | solution.py:27
  116.0 8.8 %collective-permute-start.14 = (f32[87,8,32]{2,1,0:T(8,128)S(1)}, f32[87,8,32]{2,1,0:T(8,128)}, u32[]{:S(2)}, u32[]{:S(2)}) collective-permute-start(f32[87,8,32]{2,1,0:T(8,128)S(1)} %slice.201), channel_id=1, source_target_pairs={{0,1},{1,2},{2,3},{3,4},{4,5},{5,6},{6,7},{7,0},{8,9},{9,10},{10,1... | collective-permute-start | bytes 267272 | tf_op jit(solution)/shard_map/ppermute | solution.py:21
  116.1 11.7 %collective-permute-start.17 = (f32[87,8,128]{2,1,0:T(8,128)}, f32[87,8,128]{2,1,0:T(8,128)}, u32[]{:S(2)}, u32[]{:S(2)}) collective-permute-start(f32[87,8,128]{2,1,0:T(8,128)} %get-tuple-element.26), channel_id=1, source_target_pairs={{0,16},{16,0},{1,17},{17,1},{2,18},{18,2},{3,19},{19,3},{4,20},{20... | collective-permute-start | bytes 1069064 | tf_op jit(solution)/shard_map/ppermute | solution.py:27
  127.1 8.9 %collective-permute-start.16 = (f32[87,8,16]{2,1,0:T(8,128)}, f32[87,8,16]{2,1,0:T(8,128)}, u32[]{:S(2)}, u32[]{:S(2)}) collective-permute-start(f32[87,8,16]{2,1,0:T(8,128)} %slice.203), channel_id=1, source_target_pairs={{0,1},{1,2},{2,3},{3,4},{4,5},{5,6},{6,7},{7,0},{8,9},{9,10},{10,1... | collective-permute-start | bytes 133640 | tf_op jit(solution)/shard_map/ppermute | solution.py:21
  140.1 8.7 %collective-permute-start.18 = (f32[87,8,8]{2,1,0:T(8,128)S(1)}, f32[87,8,8]{2,1,0:T(8,128)S(1)}, u32[]{:S(2)}, u32[]{:S(2)}) collective-permute-start(f32[87,8,8]{2,1,0:T(8,128)S(1)} %slice.205), channel_id=1, source_target_pairs={{0,1},{1,2},{2,3},{3,4},{4,5},{5,6},{6,7},{7,0},{8,9},{9,10},{10,1... | collective-permute-start | bytes 66824 | tf_op jit(solution)/shard_map/ppermute | solution.py:21
  140.9 10.5 %collective-permute-start.20 = (f32[87,8,128]{2,1,0:T(8,128)S(1)}, f32[87,8,128]{2,1,0:T(8,128)S(1)}, u32[]{:S(2)}, u32[]{:S(2)}) collective-permute-start(f32[87,8,128]{2,1,0:T(8,128)S(1)} %copy-done.2), channel_id=1, source_target_pairs={{0,16},{16,0},{1,17},{17,1},{2,18},{18,2},{3,19},{19,3},{4,20},{20... | collective-permute-start | bytes 1069064 | tf_op jit(solution)/shard_map/ppermute | solution.py:27
  157.0 8.7 %collective-permute-start.21 = (f32[87,8,4]{2,1,0:T(8,128)S(1)}, f32[87,8,4]{2,1,0:T(8,128)S(1)}, u32[]{:S(2)}, u32[]{:S(2)}) collective-permute-start(f32[87,8,4]{2,1,0:T(8,128)S(1)} %slice.207), channel_id=1, source_target_pairs={{0,1},{1,2},{2,3},{3,4},{4,5},{5,6},{6,7},{7,0},{8,9},{9,10},{10,1... | collective-permute-start | bytes 33416 | tf_op jit(solution)/shard_map/ppermute | solution.py:21
  157.8 14.8 %collective-permute-start.23 = (f32[87,8,128]{2,1,0:T(8,128)S(1)}, f32[87,8,128]{2,1,0:T(8,128)S(1)}, u32[]{:S(2)}, u32[]{:S(2)}) collective-permute-start(f32[87,8,128]{2,1,0:T(8,128)S(1)} %copy-done.5), channel_id=1, source_target_pairs={{0,16},{16,0},{1,17},{17,1},{2,18},{18,2},{3,19},{19,3},{4,20},{20... | collective-permute-start | bytes 1069064 | tf_op jit(solution)/shard_map/ppermute | solution.py:27
  171.1 19.2 %collective-permute-start.26 = (f32[87,8,128]{2,1,0:T(8,128)S(1)}, f32[87,8,128]{2,1,0:T(8,128)S(1)}, u32[]{:S(2)}, u32[]{:S(2)}) collective-permute-start(f32[87,8,128]{2,1,0:T(8,128)S(1)} %copy-done.4), channel_id=1, source_target_pairs={{0,16},{16,0},{1,17},{17,1},{2,18},{18,2},{3,19},{19,3},{4,20},{20... | collective-permute-start | bytes 1069064 | tf_op jit(solution)/shard_map/ppermute | solution.py:27
  174.8 8.7 %collective-permute-start.24 = (f32[87,8,2]{2,1,0:T(8,128)S(1)}, f32[87,8,2]{2,1,0:T(8,128)S(1)}, u32[]{:S(2)}, u32[]{:S(2)}) collective-permute-start(f32[87,8,2]{2,1,0:T(8,128)S(1)} %slice.211), channel_id=1, source_target_pairs={{0,1},{1,2},{2,3},{3,4},{4,5},{5,6},{6,7},{7,0},{8,9},{9,10},{10,1... | collective-permute-start | bytes 16712 | tf_op jit(solution)/shard_map/ppermute | solution.py:21
  188.1 25.5 %collective-permute-start.29 = (f32[87,8,128]{2,1,0:T(8,128)S(1)}, f32[87,8,128]{2,1,0:T(8,128)S(1)}, u32[]{:S(2)}, u32[]{:S(2)}) collective-permute-start(f32[87,8,128]{2,1,0:T(8,128)S(1)} %copy-done.3), channel_id=1, source_target_pairs={{0,16},{16,0},{1,17},{17,1},{2,18},{18,2},{3,19},{19,3},{4,20},{20... | collective-permute-start | bytes 1069064 | tf_op jit(solution)/shard_map/ppermute | solution.py:27
  191.8 8.7 %collective-permute-start.27 = (f32[87,8,1]{2,1,0:T(8,128)S(1)}, f32[87,8,1]{2,1,0:T(8,128)S(1)}, u32[]{:S(2)}, u32[]{:S(2)}) collective-permute-start(f32[87,8,1]{2,1,0:T(8,128)S(1)} %slice.215), channel_id=1, source_target_pairs={{0,1},{1,2},{2,3},{3,4},{4,5},{5,6},{6,7},{7,0},{8,9},{9,10},{10,1... | collective-permute-start | bytes 8360 | tf_op jit(solution)/shard_map/ppermute | solution.py:21
  200.6 13.0 %collective-permute-start.28 = (f32[87,1,128]{2,1,0:T(1,128)S(1)}, f32[87,1,128]{2,1,0:T(1,128)S(1)}, u32[]{:S(2)}, u32[]{:S(2)}) collective-permute-start(f32[87,1,128]{2,1,0:T(1,128)S(1)} %slice.217), channel_id=1, source_target_pairs={{0,8},{1,9},{2,10},{3,11},{4,12},{5,13},{6,14},{7,15},{16,24},{17,... | collective-permute-start | bytes 133640 | tf_op jit(solution)/shard_map/ppermute | solution.py:15
  (12 other events, 67.9 us)
where the time goes:
time: 247 us; the launch traced here: 246 us
  waiting for transfers between devices  117 us (47%)
  starting transfers between devices  53.7 us (22%)
  blocking collectives  30 us (12%)
  other arithmetic  25 us (10%)
  between operations  14.5 us (6%)
  local copies, waits for them, and re-layouts  6 us (2%)
    ppermute x14, waiting for transfers between devices, from_behind(): return lax.ppermute(value, axis, pairs)  83.3 us
    psum x1, blocking collectives, shards(): loss = lax.psum(loss_local, ('lat', 'lon'))  30 us
    ppermute x8, waiting for transfers between devices, passed_along(): return lax.ppermute(value, axis, pairs)  25.9 us
    ppermute x14, starting transfers between devices, from_behind(): return lax.ppermute(value, axis, pairs)  22.4 us
    ppermute x8, starting transfers between devices, passed_along(): return lax.ppermute(value, axis, pairs)  20 us
    ppermute x8, starting transfers between devices, from_partner(): return lax.ppermute(value, axis, pairs)  11.3 us
    reduce_sum x5, other arithmetic, shards(): jnp.sum(lat_box[:, None] * score)  9.65 us
    ppermute x8, waiting for transfers between devices, from_partner(): return lax.ppermute(value, axis, pairs)  7.88 us
  transfers between devices with their start and end apart: 30, of which 22 were waited for; matrix products, arithmetic and copies ran while one was open for 6% of the time, Pallas kernels for 0%

commit v1 on v0

v1 whole, which is shorter than its diff:
```python
import functools

import jax
import jax.numpy as jnp
import numpy as np
from jax import lax
from jax.experimental import pallas as pl
from jax.experimental.pallas import tpu as pltpu
from jax.sharding import PartitionSpec as P

LEVELS = 7
SMOOTH_EPS = 0.05
CHUNKS = 2
MESH = pl.DeviceIdType.MESH


def lat_tables(row_count):
    row_index = np.arange(row_count, dtype=np.float32)
    angle = (np.float32(89.875) - np.float32(0.25) * row_index) * np.float32(np.pi / 180.0)
    current = np.cos(angle).astype(np.float32)
    boxes = [current]
    for level in range(LEVELS):
        reach = 2**level
        current = current + np.pad(current, (0, reach))[reach : reach + row_count]
        boxes.append(current)
    return boxes


def kernel(
    sizes, factors, members_ref, target_ref, tables_ref, grad_ref, loss_ref,
    mem_v, tgt_v, tab_v, sent, field, east, own_adj, east_adj, west_adj, final,
    total, group_loss, lon_loss,
    in_sem, x_send, x_recv, h_send, h_recv, b_send, b_recv, o_send, o_recv, o_own,
    lg_send, lg_recv, ll_send, ll_recv,
):
    channels, rows, cols, bands, sectors, span, chunks = sizes
    group = 2 * bands
    quota = span * chunks
    scales = LEVELS + 1
    mem, lat, lon = lax.axis_index("mem"), lax.axis_index("lat"), lax.axis_index("lon")
    me = mem * bands + lat

    def peer(offset):
        index = lax.rem(me + offset, group)
        return index, {"mem": index // bands, "lat": lax.rem(index, bands), "lon": lon}

    def sector(offset):
        return {"mem": mem, "lat": lat, "lon": lax.rem(lon + offset, sectors)}

    loads = [
        pltpu.make_async_copy(members_ref.at[0], mem_v, in_sem.at[0]),
        pltpu.make_async_copy(target_ref, tgt_v, in_sem.at[1]),
        pltpu.make_async_copy(tables_ref, tab_v, in_sem.at[2]),
    ]
    for load in loads:
        load.start()
    barrier = pltpu.get_barrier_semaphore()
    for offset in range(1, group):
        pl.semaphore_signal(barrier, inc=1, device_id=peer(offset)[1], device_id_type=MESH)
    for offset in range(1, sectors):
        pl.semaphore_signal(barrier, inc=1, device_id=sector(offset), device_id_type=MESH)
    for load in loads:
        load.wait()

    def inverse(scale, band):
        return tab_v[scale * bands + band]

    def loss_weight(scale, band):
        return tab_v[(scales + scale) * bands + band]

    def lat_weight(band):
        return tab_v[2 * scales * bands + band]

    own_weight = tab_v[2 * scales * bands + lat]

    def remote(source, target, send, recv, device):
        return pltpu.make_async_remote_copy(
            src_ref=source, dst_ref=target, send_sem=send, recv_sem=recv,
            device_id=device, device_id_type=MESH,
        )

    exchange = []
    for k in range(chunks):
        for g in range(group):
            base = g * quota + k * span
            valid = min(max(channels - base, 0), span)
            if valid > 0:
                part = mem_v[base : base + valid] - tgt_v[base : base + valid]
                sent[k, g, 0:valid] = part * own_weight
            if valid < span:
                sent[k, g, valid:span] = jnp.zeros((span - valid, rows, cols), jnp.float32)
        if k == 0:
            pl.semaphore_wait(barrier, group + sectors - 2)
        copies = []
        for offset in range(1, group):
            index, device = peer(offset)
            copy = remote(sent.at[k, index], field.at[k, me], x_send.at[k, offset], x_recv.at[k, offset], device)
            copy.start()
            copies.append(copy)
        field[k, me] = sent[k, me]
        exchange.append(copies)

    halos = []
    for k in range(chunks):
        for copy in exchange[k]:
            copy.wait_recv()
        copy = remote(field.at[k], east.at[k], h_send.at[k], h_recv.at[k], sector(sectors - 1))
        copy.start()
        halos.append(copy)

    lane = lax.broadcasted_iota(jnp.int32, (rows, cols), 1)
    sub = lax.broadcasted_iota(jnp.int32, (rows, cols), 0)
    zero = jnp.zeros((rows, cols), jnp.float32)

    def rows_ahead(tiles, reach):
        hops, remain = divmod(reach, rows)
        if hops >= bands:
            return tiles
        at = lambda b: tiles[b] if b < bands else None
        if remain == 0:
            return [t if at(b + hops) is None else t + at(b + hops) for b, t in enumerate(tiles)]
        turned = [pltpu.roll(t, rows - remain, 0) for t in tiles]
        near = sub < rows - remain
        out = []
        for b, t in enumerate(tiles):
            if b + hops >= bands:
                out.append(t)
                continue
            beyond = turned[b + hops + 1] if b + hops + 1 < bands else zero
            out.append(t + jnp.where(near, turned[b + hops], beyond))
        return out

    def rows_behind(tiles, reach):
        hops, remain = divmod(reach, rows)
        if hops >= bands:
            return tiles
        if remain == 0:
            return [t + tiles[b - hops] if b >= hops else t for b, t in enumerate(tiles)]
        turned = [pltpu.roll(t, remain, 0) for t in tiles]
        near = sub >= remain
        out = []
        for b, t in enumerate(tiles):
            if b < hops:
                out.append(t)
                continue
            beyond = turned[b - hops - 1] if b - hops - 1 >= 0 else zero
            out.append(t + jnp.where(near, turned[b - hops], beyond))
        return out

    def absolute(value):
        square = value * value + SMOOTH_EPS * SMOOTH_EPS
        root = lax.rsqrt(square)
        return square * root, value * root

    total[...] = zero

    def work(k, i):
        own = [[field[k, m * bands + b, i] for b in range(bands)] for m in range(2)]
        next_ = [[east[k, m * bands + b, i] for b in range(bands)] for m in range(2)]
        slopes = []
        score = zero
        for scale in range(scales):
            if scale > 0:
                reach = 2 ** (scale - 1)
                own = [rows_ahead(t, reach) for t in own]
                next_ = [rows_ahead(t, reach) for t in next_]
                keep = lane < cols - reach
                for m in range(2):
                    for b in range(bands):
                        turned_own = pltpu.roll(own[m][b], cols - reach, 1)
                        turned_next = pltpu.roll(next_[m][b], cols - reach, 1)
                        own[m][b] = own[m][b] + jnp.where(keep, turned_own, turned_next)
                        if scale < LEVELS:
                            next_[m][b] = next_[m][b] + turned_next
            slope = [[], []]
            for b in range(bands):
                leader = own[0][b] * inverse(scale, b)
                partner = own[1][b] * inverse(scale, b)
                first_abs, first_slope = absolute(leader)
                second_abs, second_slope = absolute(partner)
                spread_abs, spread_slope = absolute(leader - partner)
                score = score + loss_weight(scale, b) * (first_abs + second_abs - spread_abs)
                slope[0].append((first_slope - spread_slope) * factors[scale])
                slope[1].append((second_slope + spread_slope) * factors[scale])
            slopes.append(slope)
        mine = slopes[LEVELS]
        theirs = [[zero] * bands for m in range(2)]
        for level in reversed(range(LEVELS)):
            reach = 2**level
            keep = lane >= reach
            for m in range(2):
                for b in range(bands):
                    turned_mine = pltpu.roll(mine[m][b], reach, 1)
                    if level == LEVELS - 1:
                        theirs[m][b] = jnp.where(keep, zero, turned_mine)
                    else:
                        turned_theirs = pltpu.roll(theirs[m][b], reach, 1)
                        theirs[m][b] = theirs[m][b] + jnp.where(keep, turned_theirs, turned_mine)
                    mine[m][b] = mine[m][b] + jnp.where(keep, turned_mine, zero)
            mine = [rows_behind(t, reach) for t in mine]
            theirs = [rows_behind(t, reach) for t in theirs]
            mine = [[t + s for t, s in zip(mine[m], slopes[level][m])] for m in range(2)]
        for m in range(2):
            for b in range(bands):
                own_adj[k, m * bands + b, i] = mine[m][b]
                east_adj[k, m * bands + b, i] = theirs[m][b]
        valid = (me * quota + k * span + i < channels).astype(jnp.float32)
        total[...] += score * valid

    def finish(k, back):
        back.wait_recv()
        for g in range(group):
            final[k, g] = (own_adj[k, g] + west_adj[k, g]) * lat_weight(g % bands)
        place = pl.ds(me * quota + k * span, span)
        copies = []
        for offset in range(1, group):
            index, device = peer(offset)
            copy = remote(final.at[k, index], grad_ref.at[place], o_send.at[k, offset], o_recv.at[k, offset], device)
            copy.start()
            copies.append(copy)
        stay = pltpu.make_async_copy(final.at[k, me], grad_ref.at[place], o_own.at[k])
        stay.start()
        return copies, stay

    backs, outs = [], []
    for k in range(chunks):
        halos[k].wait_recv()

        def step(i, carry, k=k):
            work(k, i)
            return carry

        lax.fori_loop(0, span, step, 0)
        back = remote(east_adj.at[k], west_adj.at[k], b_send.at[k], b_recv.at[k], sector(1))
        back.start()
        backs.append(back)
        if k > 0:
            outs.append(finish(k - 1, backs[k - 1]))

    group_loss[me] = total[...]
    group_copies = []
    for offset in range(1, group):
        copy = remote(total, group_loss.at[me], lg_send.at[offset], lg_recv.at[offset], peer(offset)[1])
        copy.start()
        group_copies.append(copy)
    outs.append(finish(chunks - 1, backs[chunks - 1]))
    for copy in group_copies:
        copy.wait()
    subtotal = group_loss[0]
    for g in range(1, group):
        subtotal = subtotal + group_loss[g]
    lon_loss[lon] = subtotal
    total[...] = subtotal
    lon_copies = []
    for offset in range(1, sectors):
        copy = remote(total, lon_loss.at[lon], ll_send.at[offset], ll_recv.at[offset], sector(offset))
        copy.start()
        lon_copies.append(copy)
    for copy in lon_copies:
        copy.wait()
    subtotal = lon_loss[0]
    for j in range(1, sectors):
        subtotal = subtotal + lon_loss[j]
    loss_ref[0, 0] = jnp.sum(subtotal)

    for copies in exchange:
        for copy in copies:
            copy.wait_send()
    for copy in halos + backs:
        copy.wait_send()
    for copies, stay in outs:
        stay.wait()
        for copy in copies:
            copy.wait()


def shards(members, target):
    channels, rows, cols = target.shape
    bands, sectors = lax.axis_size("lat"), lax.axis_size("lon")
    assert lax.axis_size("mem") == 2 and cols >= 2**LEVELS
    group = 2 * bands
    chunks = CHUNKS
    span = -(-channels // (group * chunks))
    quota = span * chunks
    scales = LEVELS + 1
    nlat, nlon = rows * bands, cols * sectors

    boxes = lat_tables(nlat)
    sums = [float(np.sum(box.astype(np.float64))) for box in boxes]
    inverses = [1.0 / (2.0**s * boxes[s].astype(np.float64)) for s in range(scales)]
    weights = [0.5 * boxes[s].astype(np.float64) / (channels * nlon * sums[s]) for s in range(scales)]
    vectors = np.stack(inverses + weights + [boxes[0].astype(np.float64)]).astype(np.float32)
    tables = np.broadcast_to(vectors.reshape(-1, rows, 1), ((2 * scales + 1) * bands, rows, cols))
    factors = [0.5 * nlat / (sums[s] * 2.0**s) for s in range(scales)]

    sizes = (channels, rows, cols, bands, sectors, span, chunks)
    blocks = pltpu.VMEM((chunks, group, span, rows, cols), jnp.float32)
    dma = pltpu.SemaphoreType.DMA
    gradient, loss = pl.pallas_call(
        functools.partial(kernel, sizes, factors),
        out_shape=(
            jax.ShapeDtypeStruct((group * quota, rows, cols), jnp.float32),
            jax.ShapeDtypeStruct((1, 1), jnp.float32),
        ),
        in_specs=[pl.BlockSpec(memory_space=pl.ANY)] * 3,
        out_specs=(pl.BlockSpec(memory_space=pl.ANY), pl.BlockSpec(memory_space=pltpu.SMEM)),
        scratch_shapes=[
            pltpu.VMEM((channels, rows, cols), jnp.float32),
            pltpu.VMEM((channels, rows, cols), jnp.float32),
            pltpu.VMEM(tables.shape, jnp.float32),
            blocks, blocks, blocks, blocks, blocks, blocks, blocks,
            pltpu.VMEM((rows, cols), jnp.float32),
            pltpu.VMEM((group, rows, cols), jnp.float32),
            pltpu.VMEM((sectors, rows, cols), jnp.float32),
            dma((3,)),
            dma((chunks, group)), dma((chunks, group)),
            dma((chunks,)), dma((chunks,)),
            dma((chunks,)), dma((chunks,)),
            dma((chunks, group)), dma((chunks, group)), dma((chunks,)),
            dma((group,)), dma((group,)),
            dma((sectors,)), dma((sectors,)),
        ],
        compiler_params=pltpu.CompilerParams(
            collective_id=0, has_side_effects=True, vmem_limit_bytes=32 * 1024 * 1024
        ),
    )(members, target, jnp.asarray(tables))
    return gradient[None, :channels], loss[0, 0]


def solution(mesh):
    return jax.shard_map(
        shards,
        mesh=mesh,
        in_specs=(P("mem", None, "lat", "lon"), P(None, "lat", "lon")),
        out_specs=(P("mem", None, "lat", "lon"), P()),
        check_vma=False,
    )
```

time: 247 us -> 54.5 us (0.22)
  waiting for transfers between devices: 117 us -> 0 us
  starting transfers between devices: 53.7 us -> 0 us
  Pallas kernels: 0 us -> 48.2 us
  blocking collectives: 30 us -> 0 us
  other arithmetic: 25 us -> 0 us
  between operations: 14.5 us -> 2.42 us
    ppermute x30 -> x0, waiting for transfers between devices: 117 us -> none  [the longest x14 83.3 us: from_behind(): return lax.ppermute(value, axis, pairs)]
    ppermute x30 -> x0, starting transfers between devices: 53.7 us -> none  [the longest x14 22.4 us: from_behind(): return lax.ppermute(value, axis, pairs)]
    pallas_call x0 -> x1, Pallas kernels: none -> 48.2 us  [shards(): pl.pallas_call(functools.partial(kernel, sizes, factors), out_shape=(jax....]
    psum x1 -> x0, blocking collectives: 30 us -> none  [shards(): loss = lax.psum(loss_local, ('lat', 'lon'))]
    reduce_sum x10 -> x0, other arithmetic: 13.1 us -> none  [the longest x5 9.65 us: shards(): jnp.sum(lat_box[:, None] * score)]
    div x4 -> x0, other arithmetic: 4.77 us -> none  [shards(): pooled = box_sum / (pool_cells * lat_box)[:, None]]
    add x10 -> x0, other arithmetic: 4.06 us -> none  [the longest x2 3.07 us: shards(): adjoint = adjoint + cotangents[level]]
    slice x16 -> x0, local copies, waits for them, and re-layouts: 3.4 us -> none  [the longest x7 2.6 us: cols_behind(): values[..., col_count - remain:]]
  transfers between devices with their start and end apart: 30 -> 0, of which waited for: 22 -> 0; matrix products, arithmetic and copies ran while one was open for 6% -> 0% of each run, Pallas kernels for 0% -> 0%
where the time goes in v1:
time: 54.5 us; the launch traced here: 54.2 us
  Pallas kernels  48.2 us (88%)
  local copies, waits for them, and re-layouts  3.54 us (6%)
  between operations  2.42 us (4%)
    pallas_call x1, Pallas kernels, shards(): pl.pallas_call(functools.partial(kernel, sizes, factors), out_shape=(jax....  48.2 us
    unnamed x4, local copies, waits for them, and re-layouts  1.96 us

profile of v1, /device:TPU:0, one launch (start us, length us, event | category | flops | bytes accessed | tf_op | source)
XLA Modules:
  0.0 54.2 jit_solution(9889603313795270948)
XLA Ops:
  0.6 0.8 %jit_solution_.3.tables_ref = f32[34,8,128]{2,1,0:T(8,128)S(1)} broadcast(f32[34,8]{1,0:T(8,128)} %constant.2.clone), dimensions={0,1} | broadcast | bytes 140352 | tf_op jit(solution)
  1.5 0.0 copy-start
  1.5 1.0 %copy-done = f32[1,87,8,128]{3,2,1,0:T(8,128)S(1)} copy-done((f32[1,87,8,128]{3,2,1,0:T(8,128)S(1)}, f32[1,87,8,128]{3,2,1,0:T(8,128)}, u32[]{:S(2)}) %copy-start) | copy-done | bytes 356376
  2.4 0.0 copy-start.1
  2.4 1.0 %copy-done.1 = f32[87,8,128]{2,1,0:T(8,128)S(1)} copy-done((f32[87,8,128]{2,1,0:T(8,128)S(1)}, f32[87,8,128]{2,1,0:T(8,128)}, u32[]{:S(2)}) %copy-start.1) | copy-done | bytes 356376
  3.4 48.2 %shard_map.50 = (f32[88,8,128]{2,1,0:T(8,128)S(1)}, f32[1,1]{1,0:T(1,128)}) custom-call(f32[1,87,8,128]{3,2,1,0:T(8,128)S(1)} %copy-done, f32[87,8,128]{2,1,0:T(8,128)S(1)} %copy-done.1, f32[34,8,128]{2,1,0:T(8,128)S(1)} %jit_solution_.3.tables_ref), custom_call_target="tpu_custom_call" | custom-call | tf_op jit(solution)/shard_map/pallas_call | solution.py:299
  51.7 0.8 %slice_bitcast_fusion = f32[1,87,8,128]{3,2,1,0:T(8,128)} fusion(f32[88,8,128]{2,1,0:T(8,128)S(1)} %get-tuple-element.4), kind=kLoop, calls=%fused_computation | loop fusion | bytes 712704 | tf_op jit(solution)/shard_map/broadcast_in_dim | solution.py:327
Async XLA Ops:
  1.5 1.0 %copy-start = (f32[1,87,8,128]{3,2,1,0:T(8,128)S(1)}, f32[1,87,8,128]{3,2,1,0:T(8,128)}, u32[]{:S(2)}) copy-start(f32[1,87,8,128]{3,2,1,0:T(8,128)} %members_ref.1) | copy-start | bytes 1069060
  2.4 1.0 %copy-start.1 = (f32[87,8,128]{2,1,0:T(8,128)S(1)}, f32[87,8,128]{2,1,0:T(8,128)}, u32[]{:S(2)}) copy-start(f32[87,8,128]{2,1,0:T(8,128)} %target_ref.1) | copy-start | bytes 1069060

commit v2 on v1

--- a/solution.py
+++ b/solution.py
@@ -27,8 +27,8 @@
 
 
 def kernel(
-    sizes, factors, members_ref, target_ref, tables_ref, grad_ref, loss_ref,
-    mem_v, tgt_v, tab_v, sent, field, east, own_adj, east_adj, west_adj, final,
+    sizes, factors, vectors, members_ref, target_ref, grad_ref, loss_ref,
+    mem_v, tgt_v, tab_v, slopes, sent, field, east, own_adj, east_adj, west_adj, final,
     total, group_loss, lon_loss,
     in_sem, x_send, x_recv, h_send, h_recv, b_send, b_recv, o_send, o_recv, o_own,
     lg_send, lg_recv, ll_send, ll_recv,
@@ -50,7 +50,6 @@
     loads = [
         pltpu.make_async_copy(members_ref.at[0], mem_v, in_sem.at[0]),
         pltpu.make_async_copy(target_ref, tgt_v, in_sem.at[1]),
-        pltpu.make_async_copy(tables_ref, tab_v, in_sem.at[2]),
     ]
     for load in loads:
         load.start()
@@ -59,6 +58,15 @@
         pl.semaphore_signal(barrier, inc=1, device_id=peer(offset)[1], device_id_type=MESH)
     for offset in range(1, sectors):
         pl.semaphore_signal(barrier, inc=1, device_id=sector(offset), device_id_type=MESH)
+
+    lane = lax.broadcasted_iota(jnp.int32, (rows, cols), 1)
+    sub = lax.broadcasted_iota(jnp.int32, (rows, cols), 0)
+    zero = jnp.zeros((rows, cols), jnp.float32)
+    for i, vector in enumerate(vectors):
+        tile = jnp.full((rows, cols), vector[0], jnp.float32)
+        for r in range(1, rows):
+            tile = jnp.where(sub == r, vector[r], tile)
+        tab_v[i] = tile
     for load in loads:
         load.wait()
 
@@ -108,10 +116,6 @@
         copy.start()
         halos.append(copy)
 
-    lane = lax.broadcasted_iota(jnp.int32, (rows, cols), 1)
-    sub = lax.broadcasted_iota(jnp.int32, (rows, cols), 0)
-    zero = jnp.zeros((rows, cols), jnp.float32)
-
     def rows_ahead(tiles, reach):
         hops, remain = divmod(reach, rows)
         if hops >= bands:
@@ -119,7 +123,7 @@
         at = lambda b: tiles[b] if b < bands else None
         if remain == 0:
             return [t if at(b + hops) is None else t + at(b + hops) for b, t in enumerate(tiles)]
-        turned = [pltpu.roll(t, rows - remain, 0) for t in tiles]
+        turned = [pltpu.roll(t, rows - remain, 1) for t in tiles]
         near = sub < rows - remain
         out = []
         for b, t in enumerate(tiles):
@@ -136,7 +140,7 @@
             return tiles
         if remain == 0:
             return [t + tiles[b - hops] if b >= hops else t for b, t in enumerate(tiles)]
-        turned = [pltpu.roll(t, remain, 0) for t in tiles]
+        turned = [pltpu.roll(t, remain, 1) for t in tiles]
         near = sub >= remain
         out = []
         for b, t in enumerate(tiles):
@@ -154,11 +158,10 @@
 
     total[...] = zero
 
-    def work(k, i):
-        own = [[field[k, m * bands + b, i] for b in range(bands)] for m in range(2)]
-        next_ = [[east[k, m * bands + b, i] for b in range(bands)] for m in range(2)]
-        slopes = []
-        score = zero
+    def work(k):
+        own = [[field[k, m * bands + b] for b in range(bands)] for m in range(2)]
+        next_ = [[east[k, m * bands + b] for b in range(bands)] for m in range(2)]
+        score = jnp.zeros((span, rows, cols), jnp.float32)
         for scale in range(scales):
             if scale > 0:
                 reach = 2 ** (scale - 1)
@@ -167,12 +170,11 @@
                 keep = lane < cols - reach
                 for m in range(2):
                     for b in range(bands):
-                        turned_own = pltpu.roll(own[m][b], cols - reach, 1)
-                        turned_next = pltpu.roll(next_[m][b], cols - reach, 1)
+                        turned_own = pltpu.roll(own[m][b], cols - reach, 2)
+                        turned_next = pltpu.roll(next_[m][b], cols - reach, 2)
                         own[m][b] = own[m][b] + jnp.where(keep, turned_own, turned_next)
                         if scale < LEVELS:
                             next_[m][b] = next_[m][b] + turned_next
-            slope = [[], []]
             for b in range(bands):
                 leader = own[0][b] * inverse(scale, b)
                 partner = own[1][b] * inverse(scale, b)
@@ -180,32 +182,37 @@
                 second_abs, second_slope = absolute(partner)
                 spread_abs, spread_slope = absolute(leader - partner)
                 score = score + loss_weight(scale, b) * (first_abs + second_abs - spread_abs)
-                slope[0].append((first_slope - spread_slope) * factors[scale])
-                slope[1].append((second_slope + spread_slope) * factors[scale])
-            slopes.append(slope)
-        mine = slopes[LEVELS]
-        theirs = [[zero] * bands for m in range(2)]
+                slopes[scale, b] = (first_slope - spread_slope) * factors[scale]
+                slopes[scale, bands + b] = (second_slope + spread_slope) * factors[scale]
+        mine = [[slopes[LEVELS, m * bands + b] for b in range(bands)] for m in range(2)]
+        theirs = [[None] * bands for m in range(2)]
         for level in reversed(range(LEVELS)):
             reach = 2**level
             keep = lane >= reach
             for m in range(2):
                 for b in range(bands):
-                    turned_mine = pltpu.roll(mine[m][b], reach, 1)
+                    turned_mine = pltpu.roll(mine[m][b], reach, 2)
                     if level == LEVELS - 1:
                         theirs[m][b] = jnp.where(keep, zero, turned_mine)
                     else:
-                        turned_theirs = pltpu.roll(theirs[m][b], reach, 1)
+                        turned_theirs = pltpu.roll(theirs[m][b], reach, 2)
                         theirs[m][b] = theirs[m][b] + jnp.where(keep, turned_theirs, turned_mine)
                     mine[m][b] = mine[m][b] + jnp.where(keep, turned_mine, zero)
             mine = [rows_behind(t, reach) for t in mine]
             theirs = [rows_behind(t, reach) for t in theirs]
-            mine = [[t + s for t, s in zip(mine[m], slopes[level][m])] for m in range(2)]
+            mine = [[mine[m][b] + slopes[level, m * bands + b] for b in range(bands)] for m in range(2)]
         for m in range(2):
             for b in range(bands):
-                own_adj[k, m * bands + b, i] = mine[m][b]
-                east_adj[k, m * bands + b, i] = theirs[m][b]
-        valid = (me * quota + k * span + i < channels).astype(jnp.float32)
-        total[...] += score * valid
+                own_adj[k, m * bands + b] = mine[m][b]
+                east_adj[k, m * bands + b] = theirs[m][b]
+        part = zero
+        for i in range(span):
+            place = k * span + i
+            if (group - 1) * quota + place < channels:
+                part = part + score[i]
+            else:
+                part = part + score[i] * (me * quota + place < channels).astype(jnp.float32)
+        total[...] += part
 
     def finish(k, back):
         back.wait_recv()
@@ -226,11 +233,7 @@
     for k in range(chunks):
         halos[k].wait_recv()
 
-        def step(i, carry, k=k):
-            work(k, i)
-            return carry
-
-        lax.fori_loop(0, span, step, 0)
+        work(k)
         back = remote(east_adj.at[k], west_adj.at[k], b_send.at[k], b_recv.at[k], sector(1))
         back.start()
         backs.append(back)
@@ -289,30 +292,30 @@
     sums = [float(np.sum(box.astype(np.float64))) for box in boxes]
     inverses = [1.0 / (2.0**s * boxes[s].astype(np.float64)) for s in range(scales)]
     weights = [0.5 * boxes[s].astype(np.float64) / (channels * nlon * sums[s]) for s in range(scales)]
-    vectors = np.stack(inverses + weights + [boxes[0].astype(np.float64)]).astype(np.float32)
-    tables = np.broadcast_to(vectors.reshape(-1, rows, 1), ((2 * scales + 1) * bands, rows, cols))
+    vectors = np.stack(inverses + weights + [boxes[0].astype(np.float64)]).reshape(-1, rows).tolist()
     factors = [0.5 * nlat / (sums[s] * 2.0**s) for s in range(scales)]
 
     sizes = (channels, rows, cols, bands, sectors, span, chunks)
     blocks = pltpu.VMEM((chunks, group, span, rows, cols), jnp.float32)
     dma = pltpu.SemaphoreType.DMA
     gradient, loss = pl.pallas_call(
-        functools.partial(kernel, sizes, factors),
+        functools.partial(kernel, sizes, factors, vectors),
         out_shape=(
             jax.ShapeDtypeStruct((group * quota, rows, cols), jnp.float32),
             jax.ShapeDtypeStruct((1, 1), jnp.float32),
         ),
-        in_specs=[pl.BlockSpec(memory_space=pl.ANY)] * 3,
+        in_specs=[pl.BlockSpec(memory_space=pl.ANY)] * 2,
         out_specs=(pl.BlockSpec(memory_space=pl.ANY), pl.BlockSpec(memory_space=pltpu.SMEM)),
         scratch_shapes=[
             pltpu.VMEM((channels, rows, cols), jnp.float32),
             pltpu.VMEM((channels, rows, cols), jnp.float32),
-            pltpu.VMEM(tables.shape, jnp.float32),
+            pltpu.VMEM((len(vectors), rows, cols), jnp.float32),
+            pltpu.VMEM((scales, group, span, rows, cols), jnp.float32),
             blocks, blocks, blocks, blocks, blocks, blocks, blocks,
             pltpu.VMEM((rows, cols), jnp.float32),
             pltpu.VMEM((group, rows, cols), jnp.float32),
             pltpu.VMEM((sectors, rows, cols), jnp.float32),
-            dma((3,)),
+            dma((2,)),
             dma((chunks, group)), dma((chunks, group)),
             dma((chunks,)), dma((chunks,)),
             dma((chunks,)), dma((chunks,)),
@@ -321,9 +324,9 @@
             dma((sectors,)), dma((sectors,)),
         ],
         compiler_params=pltpu.CompilerParams(
-            collective_id=0, has_side_effects=True, vmem_limit_bytes=32 * 1024 * 1024
+            collective_id=0, has_side_effects=True, vmem_limit_bytes=60 * 1024 * 1024
         ),
-    )(members, target, jnp.asarray(tables))
+    )(members, target)
     return gradient[None, :channels], loss[0, 0]
 
 

time: 54.5 us -> 33.5 us (0.61)
  Pallas kernels: 48.2 us -> 29.2 us
  local copies, waits for them, and re-layouts: 3.54 us -> 1.74 us
    pallas_call x1, Pallas kernels: 48.2 us -> 29.2 us  [shards(): pl.pallas_call(functools.partial(kernel, sizes, factors, vectors), out_sh...]
    unnamed x4 -> x0, local copies, waits for them, and re-layouts: 1.96 us -> none
    broadcast_in_dim x1, local copies, waits for them, and re-layouts: 0.76 us -> 1.74 us  [shards(): return (gradient[None, :channels], loss[0, 0])]
    another operation x1 -> x0, local copies, waits for them, and re-layouts: 0.82 us -> none
where the time goes in v2:
time: 33.5 us; the launch traced here: 33.3 us
  Pallas kernels  29.2 us (87%)
  between operations  2.4 us (7%)
  local copies, waits for them, and re-layouts  1.74 us (5%)
    pallas_call x1, Pallas kernels, shards(): pl.pallas_call(functools.partial(kernel, sizes, factors, vectors), out_sh...  29.2 us
    broadcast_in_dim x1, local copies, waits for them, and re-layouts, shards(): return (gradient[None, :channels], loss[0, 0])  1.74 us

profile of v2, /device:TPU:0, one launch (start us, length us, event | category | flops | bytes accessed | tf_op | source)
XLA Modules:
  0.0 33.3 jit_solution(11140822474170324389)
XLA Ops:
  0.6 29.2 %shard_map.41 = (f32[88,8,128]{2,1,0:T(8,128)}, f32[1,1]{1,0:T(1,128)}) custom-call(f32[1,87,8,128]{3,2,1,0:T(8,128)} %members_ref.1, f32[87,8,128]{2,1,0:T(8,128)} %target_ref.1), custom_call_target="tpu_custom_call" | custom-call | tf_op jit(solution)/shard_map/pallas_call | solution.py:301
  29.8 1.7 %slice_bitcast_fusion = f32[1,87,8,128]{3,2,1,0:T(8,128)} fusion(f32[88,8,128]{2,1,0:T(8,128)} %get-tuple-element.4), kind=kLoop, calls=%fused_computation | loop fusion | bytes 712704 | tf_op jit(solution)/shard_map/broadcast_in_dim | solution.py:330

commit v3 on v2

--- a/solution.py
+++ b/solution.py
@@ -10,7 +10,7 @@
 
 LEVELS = 7
 SMOOTH_EPS = 0.05
-CHUNKS = 2
+CHUNKS = 4
 MESH = pl.DeviceIdType.MESH
 
 
@@ -33,9 +33,12 @@
     in_sem, x_send, x_recv, h_send, h_recv, b_send, b_recv, o_send, o_recv, o_own,
     lg_send, lg_recv, ll_send, ll_recv,
 ):
-    channels, rows, cols, bands, sectors, span, chunks = sizes
+    channels, rows, cols, bands, sectors, spans = sizes
     group = 2 * bands
-    quota = span * chunks
+    quota = sum(spans)
+    chunks = len(spans)
+    starts = [sum(spans[:k]) for k in range(chunks)]
+    part = [pl.ds(start, span) for start, span in zip(starts, spans)]
     scales = LEVELS + 1
     mem, lat, lon = lax.axis_index("mem"), lax.axis_index("lat"), lax.axis_index("lon")
     me = mem * bands + lat
@@ -90,29 +93,30 @@
     exchange = []
     for k in range(chunks):
         for g in range(group):
-            base = g * quota + k * span
-            valid = min(max(channels - base, 0), span)
+            base = g * quota + starts[k]
+            valid = min(max(channels - base, 0), spans[k])
+            edge, stop = starts[k] + valid, starts[k] + spans[k]
             if valid > 0:
-                part = mem_v[base : base + valid] - tgt_v[base : base + valid]
-                sent[k, g, 0:valid] = part * own_weight
-            if valid < span:
-                sent[k, g, valid:span] = jnp.zeros((span - valid, rows, cols), jnp.float32)
+                difference = mem_v[base : base + valid] - tgt_v[base : base + valid]
+                sent[g, starts[k] : edge] = difference * own_weight
+            if edge < stop:
+                sent[g, edge:stop] = jnp.zeros((stop - edge, rows, cols), jnp.float32)
         if k == 0:
             pl.semaphore_wait(barrier, group + sectors - 2)
         copies = []
         for offset in range(1, group):
             index, device = peer(offset)
-            copy = remote(sent.at[k, index], field.at[k, me], x_send.at[k, offset], x_recv.at[k, offset], device)
+            copy = remote(sent.at[index, part[k]], field.at[me, part[k]], x_send.at[k, offset], x_recv.at[k, offset], device)
             copy.start()
             copies.append(copy)
-        field[k, me] = sent[k, me]
+        field[me, part[k]] = sent[me, part[k]]
         exchange.append(copies)
 
     halos = []
     for k in range(chunks):
         for copy in exchange[k]:
             copy.wait_recv()
-        copy = remote(field.at[k], east.at[k], h_send.at[k], h_recv.at[k], sector(sectors - 1))
+        copy = remote(field.at[:, part[k]], east.at[:, part[k]], h_send.at[k], h_recv.at[k], sector(sectors - 1))
         copy.start()
         halos.append(copy)
 
@@ -159,8 +163,9 @@
     total[...] = zero
 
     def work(k):
-        own = [[field[k, m * bands + b] for b in range(bands)] for m in range(2)]
-        next_ = [[east[k, m * bands + b] for b in range(bands)] for m in range(2)]
+        span = spans[k]
+        own = [[field[m * bands + b, part[k]] for b in range(bands)] for m in range(2)]
+        next_ = [[east[m * bands + b, part[k]] for b in range(bands)] for m in range(2)]
         score = jnp.zeros((span, rows, cols), jnp.float32)
         for scale in range(scales):
             if scale > 0:
@@ -182,9 +187,9 @@
                 second_abs, second_slope = absolute(partner)
                 spread_abs, spread_slope = absolute(leader - partner)
                 score = score + loss_weight(scale, b) * (first_abs + second_abs - spread_abs)
-                slopes[scale, b] = (first_slope - spread_slope) * factors[scale]
-                slopes[scale, bands + b] = (second_slope + spread_slope) * factors[scale]
-        mine = [[slopes[LEVELS, m * bands + b] for b in range(bands)] for m in range(2)]
+                slopes[scale, b, 0:span] = (first_slope - spread_slope) * factors[scale]
+                slopes[scale, bands + b, 0:span] = (second_slope + spread_slope) * factors[scale]
+        mine = [[slopes[LEVELS, m * bands + b, 0:span] for b in range(bands)] for m in range(2)]
         theirs = [[None] * bands for m in range(2)]
         for level in reversed(range(LEVELS)):
             reach = 2**level
@@ -200,32 +205,32 @@
                     mine[m][b] = mine[m][b] + jnp.where(keep, turned_mine, zero)
             mine = [rows_behind(t, reach) for t in mine]
             theirs = [rows_behind(t, reach) for t in theirs]
-            mine = [[mine[m][b] + slopes[level, m * bands + b] for b in range(bands)] for m in range(2)]
+            mine = [[mine[m][b] + slopes[level, m * bands + b, 0:span] for b in range(bands)] for m in range(2)]
         for m in range(2):
             for b in range(bands):
-                own_adj[k, m * bands + b] = mine[m][b]
-                east_adj[k, m * bands + b] = theirs[m][b]
-        part = zero
+                own_adj[m * bands + b, part[k]] = mine[m][b]
+                east_adj[m * bands + b, part[k]] = theirs[m][b]
+        kept = zero
         for i in range(span):
-            place = k * span + i
+            place = starts[k] + i
             if (group - 1) * quota + place < channels:
-                part = part + score[i]
+                kept = kept + score[i]
             else:
-                part = part + score[i] * (me * quota + place < channels).astype(jnp.float32)
-        total[...] += part
+                kept = kept + score[i] * (me * quota + place < channels).astype(jnp.float32)
+        total[...] += kept
 
     def finish(k, back):
         back.wait_recv()
         for g in range(group):
-            final[k, g] = (own_adj[k, g] + west_adj[k, g]) * lat_weight(g % bands)
-        place = pl.ds(me * quota + k * span, span)
+            final[g, part[k]] = (own_adj[g, part[k]] + west_adj[g, part[k]]) * lat_weight(g % bands)
+        place = pl.ds(me * quota + starts[k], spans[k])
         copies = []
         for offset in range(1, group):
             index, device = peer(offset)
-            copy = remote(final.at[k, index], grad_ref.at[place], o_send.at[k, offset], o_recv.at[k, offset], device)
+            copy = remote(final.at[index, part[k]], grad_ref.at[place], o_send.at[k, offset], o_recv.at[k, offset], device)
             copy.start()
             copies.append(copy)
-        stay = pltpu.make_async_copy(final.at[k, me], grad_ref.at[place], o_own.at[k])
+        stay = pltpu.make_async_copy(final.at[me, part[k]], grad_ref.at[place], o_own.at[k])
         stay.start()
         return copies, stay
 
@@ -234,7 +239,7 @@
         halos[k].wait_recv()
 
         work(k)
-        back = remote(east_adj.at[k], west_adj.at[k], b_send.at[k], b_recv.at[k], sector(1))
+        back = remote(east_adj.at[:, part[k]], west_adj.at[:, part[k]], b_send.at[k], b_recv.at[k], sector(1))
         back.start()
         backs.append(back)
         if k > 0:
@@ -282,9 +287,9 @@
     bands, sectors = lax.axis_size("lat"), lax.axis_size("lon")
     assert lax.axis_size("mem") == 2 and cols >= 2**LEVELS
     group = 2 * bands
-    chunks = CHUNKS
-    span = -(-channels // (group * chunks))
-    quota = span * chunks
+    quota = -(-channels // group)
+    chunks = min(CHUNKS, quota)
+    spans = [(quota + k) // chunks for k in range(chunks)]
     scales = LEVELS + 1
     nlat, nlon = rows * bands, cols * sectors
 
@@ -295,8 +300,8 @@
     vectors = np.stack(inverses + weights + [boxes[0].astype(np.float64)]).reshape(-1, rows).tolist()
     factors = [0.5 * nlat / (sums[s] * 2.0**s) for s in range(scales)]
 
-    sizes = (channels, rows, cols, bands, sectors, span, chunks)
-    blocks = pltpu.VMEM((chunks, group, span, rows, cols), jnp.float32)
+    sizes = (channels, rows, cols, bands, sectors, spans)
+    blocks = pltpu.VMEM((group, quota, rows, cols), jnp.float32)
     dma = pltpu.SemaphoreType.DMA
     gradient, loss = pl.pallas_call(
         functools.partial(kernel, sizes, factors, vectors),
@@ -304,13 +309,13 @@
             jax.ShapeDtypeStruct((group * quota, rows, cols), jnp.float32),
             jax.ShapeDtypeStruct((1, 1), jnp.float32),
         ),
-        in_specs=[pl.BlockSpec(memory_space=pl.ANY)] * 2,
+        in_specs=[pl.BlockSpec(memory_space=pltpu.HBM)] * 2,
         out_specs=(pl.BlockSpec(memory_space=pl.ANY), pl.BlockSpec(memory_space=pltpu.SMEM)),
         scratch_shapes=[
             pltpu.VMEM((channels, rows, cols), jnp.float32),
             pltpu.VMEM((channels, rows, cols), jnp.float32),
             pltpu.VMEM((len(vectors), rows, cols), jnp.float32),
-            pltpu.VMEM((scales, group, span, rows, cols), jnp.float32),
+            pltpu.VMEM((scales, group, max(spans), rows, cols), jnp.float32),
             blocks, blocks, blocks, blocks, blocks, blocks, blocks,
             pltpu.VMEM((rows, cols), jnp.float32),
             pltpu.VMEM((group, rows, cols), jnp.float32),
@@ -324,7 +329,7 @@
             dma((sectors,)), dma((sectors,)),
         ],
         compiler_params=pltpu.CompilerParams(
-            collective_id=0, has_side_effects=True, vmem_limit_bytes=60 * 1024 * 1024
+            collective_id=0, has_side_effects=True, vmem_limit_bytes=32 * 1024 * 1024
         ),
     )(members, target)
     return gradient[None, :channels], loss[0, 0]

time: 33.5 us -> 34.7 us (1.036)
  local copies, waits for them, and re-layouts: 1.74 us -> 2.72 us
    unnamed x0 -> x4, local copies, waits for them, and re-layouts: none -> 1.96 us
    broadcast_in_dim x1, local copies, waits for them, and re-layouts: 1.74 us -> 0.76 us  [shards(): return (gradient[None, :channels], loss[0, 0])]
where the time goes in v3:
time: 34.7 us; the launch traced here: 34.5 us
  Pallas kernels  29.4 us (85%)
  local copies, waits for them, and re-layouts  2.72 us (8%)
  between operations  2.41 us (7%)
    pallas_call x1, Pallas kernels, shards(): pl.pallas_call(functools.partial(kernel, sizes, factors, vectors), out_sh...  29.4 us
    unnamed x4, local copies, waits for them, and re-layouts  1.96 us
    broadcast_in_dim x1, local copies, waits for them, and re-layouts, shards(): return (gradient[None, :channels], loss[0, 0])  0.76 us

profile of v3, /device:TPU:0, one launch (start us, length us, event | category | flops | bytes accessed | tf_op | source)
XLA Modules:
  0.0 34.5 jit_solution(6744015596633346896)
XLA Ops:
  0.6 0.0 copy-start
  0.6 1.0 %copy-done = f32[1,87,8,128]{3,2,1,0:T(8,128)S(1)} copy-done((f32[1,87,8,128]{3,2,1,0:T(8,128)S(1)}, f32[1,87,8,128]{3,2,1,0:T(8,128)}, u32[]{:S(2)}) %copy-start) | copy-done | bytes 356376
  1.6 0.0 copy-start.1
  1.6 1.0 %copy-done.1 = f32[87,8,128]{2,1,0:T(8,128)S(1)} copy-done((f32[87,8,128]{2,1,0:T(8,128)S(1)}, f32[87,8,128]{2,1,0:T(8,128)}, u32[]{:S(2)}) %copy-start.1) | copy-done | bytes 356376
  2.6 29.4 %shard_map.41 = (f32[88,8,128]{2,1,0:T(8,128)S(1)}, f32[1,1]{1,0:T(1,128)}) custom-call(f32[1,87,8,128]{3,2,1,0:T(8,128)S(1)} %copy-done, f32[87,8,128]{2,1,0:T(8,128)S(1)} %copy-done.1), custom_call_target="tpu_custom_call" | custom-call | tf_op jit(solution)/shard_map/pallas_call | solution.py:306
  32.0 0.8 %slice_bitcast_fusion = f32[1,87,8,128]{3,2,1,0:T(8,128)} fusion(f32[88,8,128]{2,1,0:T(8,128)S(1)} %get-tuple-element.4), kind=kLoop, calls=%fused_computation | loop fusion | bytes 712704 | tf_op jit(solution)/shard_map/broadcast_in_dim | solution.py:335
Async XLA Ops:
  0.6 1.0 %copy-start = (f32[1,87,8,128]{3,2,1,0:T(8,128)S(1)}, f32[1,87,8,128]{3,2,1,0:T(8,128)}, u32[]{:S(2)}) copy-start(f32[1,87,8,128]{3,2,1,0:T(8,128)} %members_ref.1) | copy-start | bytes 1069060
  1.6 1.0 %copy-start.1 = (f32[87,8,128]{2,1,0:T(8,128)S(1)}, f32[87,8,128]{2,1,0:T(8,128)}, u32[]{:S(2)}) copy-start(f32[87,8,128]{2,1,0:T(8,128)} %target_ref.1) | copy-start | bytes 1069060

commit v4 on v2

--- a/solution.py
+++ b/solution.py
@@ -36,6 +36,9 @@
     channels, rows, cols, bands, sectors, span, chunks = sizes
     group = 2 * bands
     quota = span * chunks
+
+    def part(k):
+        return pl.ds(k * span, span)
     scales = LEVELS + 1
     mem, lat, lon = lax.axis_index("mem"), lax.axis_index("lat"), lax.axis_index("lon")
     me = mem * bands + lat
@@ -87,34 +90,46 @@
             device_id=device, device_id_type=MESH,
         )
 
-    exchange = []
+    def exchange(k, offset):
+        index, device = peer(offset)
+        return remote(sent.at[index, part(k)], field.at[me, part(k)], x_send.at[k, offset], x_recv.at[k, offset], device)
+
+    def halo(k):
+        return remote(field.at[:, part(k)], east.at[:, part(k)], h_send.at[k], h_recv.at[k], sector(sectors - 1))
+
+    def back(k):
+        return remote(east_adj.at[:, part(k)], west_adj.at[:, part(k)], b_send.at[k], b_recv.at[k], sector(1))
+
+    def place(k):
+        return grad_ref.at[pl.ds(me * quota + k * span, span)]
+
+    def result(k, offset):
+        index, device = peer(offset)
+        return remote(final.at[index, part(k)], place(k), o_send.at[k, offset], o_recv.at[k, offset], device)
+
+    def stay(k):
+        return pltpu.make_async_copy(final.at[me, part(k)], place(k), o_own.at[k])
+
     for k in range(chunks):
         for g in range(group):
             base = g * quota + k * span
             valid = min(max(channels - base, 0), span)
+            edge, stop = k * span + valid, (k + 1) * span
             if valid > 0:
-                part = mem_v[base : base + valid] - tgt_v[base : base + valid]
-                sent[k, g, 0:valid] = part * own_weight
-            if valid < span:
-                sent[k, g, valid:span] = jnp.zeros((span - valid, rows, cols), jnp.float32)
+                difference = mem_v[base : base + valid] - tgt_v[base : base + valid]
+                sent[g, k * span : edge] = difference * own_weight
+            if edge < stop:
+                sent[g, edge:stop] = jnp.zeros((stop - edge, rows, cols), jnp.float32)
         if k == 0:
             pl.semaphore_wait(barrier, group + sectors - 2)
-        copies = []
         for offset in range(1, group):
-            index, device = peer(offset)
-            copy = remote(sent.at[k, index], field.at[k, me], x_send.at[k, offset], x_recv.at[k, offset], device)
-            copy.start()
-            copies.append(copy)
-        field[k, me] = sent[k, me]
-        exchange.append(copies)
-
-    halos = []
+            exchange(k, offset).start()
+        field[me, part(k)] = sent[me, part(k)]
+
     for k in range(chunks):
-        for copy in exchange[k]:
-            copy.wait_recv()
-        copy = remote(field.at[k], east.at[k], h_send.at[k], h_recv.at[k], sector(sectors - 1))
-        copy.start()
-        halos.append(copy)
+        for offset in range(1, group):
+            exchange(k, offset).wait_recv()
+        halo(k).start()
 
     def rows_ahead(tiles, reach):
         hops, remain = divmod(reach, rows)
@@ -159,8 +174,8 @@
     total[...] = zero
 
     def work(k):
-        own = [[field[k, m * bands + b] for b in range(bands)] for m in range(2)]
-        next_ = [[east[k, m * bands + b] for b in range(bands)] for m in range(2)]
+        own = [[field[m * bands + b, part(k)] for b in range(bands)] for m in range(2)]
+        next_ = [[east[m * bands + b, part(k)] for b in range(bands)] for m in range(2)]
         score = jnp.zeros((span, rows, cols), jnp.float32)
         for scale in range(scales):
             if scale > 0:
@@ -182,9 +197,9 @@
                 second_abs, second_slope = absolute(partner)
                 spread_abs, spread_slope = absolute(leader - partner)
                 score = score + loss_weight(scale, b) * (first_abs + second_abs - spread_abs)
-                slopes[scale, b] = (first_slope - spread_slope) * factors[scale]
-                slopes[scale, bands + b] = (second_slope + spread_slope) * factors[scale]
-        mine = [[slopes[LEVELS, m * bands + b] for b in range(bands)] for m in range(2)]
+                slopes[scale, b, 0:span] = (first_slope - spread_slope) * factors[scale]
+                slopes[scale, bands + b, 0:span] = (second_slope + spread_slope) * factors[scale]
+        mine = [[slopes[LEVELS, m * bands + b, 0:span] for b in range(bands)] for m in range(2)]
         theirs = [[None] * bands for m in range(2)]
         for level in reversed(range(LEVELS)):
             reach = 2**level
@@ -200,45 +215,36 @@
                     mine[m][b] = mine[m][b] + jnp.where(keep, turned_mine, zero)
             mine = [rows_behind(t, reach) for t in mine]
             theirs = [rows_behind(t, reach) for t in theirs]
-            mine = [[mine[m][b] + slopes[level, m * bands + b] for b in range(bands)] for m in range(2)]
+            mine = [[mine[m][b] + slopes[level, m * bands + b, 0:span] for b in range(bands)] for m in range(2)]
         for m in range(2):
             for b in range(bands):
-                own_adj[k, m * bands + b] = mine[m][b]
-                east_adj[k, m * bands + b] = theirs[m][b]
-        part = zero
+                own_adj[m * bands + b, part(k)] = mine[m][b]
+                east_adj[m * bands + b, part(k)] = theirs[m][b]
+        kept = zero
         for i in range(span):
-            place = k * span + i
-            if (group - 1) * quota + place < channels:
-                part = part + score[i]
-            else:
-                part = part + score[i] * (me * quota + place < channels).astype(jnp.float32)
-        total[...] += part
-
-    def finish(k, back):
-        back.wait_recv()
+            kept = kept + score[i] * (me * quota + k * span + i < channels).astype(jnp.float32)
+        total[...] += kept
+
+    def finish(k):
+        back(k).wait_recv()
         for g in range(group):
-            final[k, g] = (own_adj[k, g] + west_adj[k, g]) * lat_weight(g % bands)
-        place = pl.ds(me * quota + k * span, span)
-        copies = []
+            final[g, part(k)] = (own_adj[g, part(k)] + west_adj[g, part(k)]) * lat_weight(g % bands)
         for offset in range(1, group):
-            index, device = peer(offset)
-            copy = remote(final.at[k, index], grad_ref.at[place], o_send.at[k, offset], o_recv.at[k, offset], device)
-            copy.start()
-            copies.append(copy)
-        stay = pltpu.make_async_copy(final.at[k, me], grad_ref.at[place], o_own.at[k])
-        stay.start()
-        return copies, stay
-
-    backs, outs = [], []
-    for k in range(chunks):
-        halos[k].wait_recv()
-
+            result(k, offset).start()
+        stay(k).start()
+
+    def turn(k, carry):
+        halo(k).wait_recv()
         work(k)
-        back = remote(east_adj.at[k], west_adj.at[k], b_send.at[k], b_recv.at[k], sector(1))
-        back.start()
-        backs.append(back)
-        if k > 0:
-            outs.append(finish(k - 1, backs[k - 1]))
+        back(k).start()
+
+        @pl.when(k > 0)
+        def _():
+            finish(k - 1)
+
+        return carry
+
+    lax.fori_loop(0, chunks, turn, 0)
 
     group_loss[me] = total[...]
     group_copies = []
@@ -246,7 +252,7 @@
         copy = remote(total, group_loss.at[me], lg_send.at[offset], lg_recv.at[offset], peer(offset)[1])
         copy.start()
         group_copies.append(copy)
-    outs.append(finish(chunks - 1, backs[chunks - 1]))
+    finish(chunks - 1)
     for copy in group_copies:
         copy.wait()
     subtotal = group_loss[0]
@@ -266,15 +272,13 @@
         subtotal = subtotal + lon_loss[j]
     loss_ref[0, 0] = jnp.sum(subtotal)
 
-    for copies in exchange:
-        for copy in copies:
-            copy.wait_send()
-    for copy in halos + backs:
-        copy.wait_send()
-    for copies, stay in outs:
-        stay.wait()
-        for copy in copies:
-            copy.wait()
+    for k in range(chunks):
+        halo(k).wait_send()
+        back(k).wait_send()
+        stay(k).wait()
+        for offset in range(1, group):
+            exchange(k, offset).wait_send()
+            result(k, offset).wait()
 
 
 def shards(members, target):
@@ -296,7 +300,7 @@
     factors = [0.5 * nlat / (sums[s] * 2.0**s) for s in range(scales)]
 
     sizes = (channels, rows, cols, bands, sectors, span, chunks)
-    blocks = pltpu.VMEM((chunks, group, span, rows, cols), jnp.float32)
+    blocks = pltpu.VMEM((group, quota, rows, cols), jnp.float32)
     dma = pltpu.SemaphoreType.DMA
     gradient, loss = pl.pallas_call(
         functools.partial(kernel, sizes, factors, vectors),

time: 33.5 us -> 33.5 us (level)
  no operation moved by 1% of the time
where the time goes in v4:
time: 33.5 us; the launch traced here: 33.3 us
  Pallas kernels  29.2 us (87%)
  between operations  2.4 us (7%)
  local copies, waits for them, and re-layouts  1.74 us (5%)
    pallas_call x1, Pallas kernels, shards(): pl.pallas_call(functools.partial(kernel, sizes, factors, vectors), out_sh...  29.2 us
    broadcast_in_dim x1, local copies, waits for them, and re-layouts, shards(): return (gradient[None, :channels], loss[0, 0])  1.74 us

profile of v4, /device:TPU:0, one launch (start us, length us, event | category | flops | bytes accessed | tf_op | source)
XLA Modules:
  0.0 33.3 jit_solution(18217152286164228432)
XLA Ops:
  0.6 29.2 %shard_map.41 = (f32[88,8,128]{2,1,0:T(8,128)}, f32[1,1]{1,0:T(1,128)}) custom-call(f32[1,87,8,128]{3,2,1,0:T(8,128)} %members_ref.1, f32[87,8,128]{2,1,0:T(8,128)} %target_ref.1), custom_call_target="tpu_custom_call" | custom-call | tf_op jit(solution)/shard_map/pallas_call | solution.py:305
  29.8 1.7 %slice_bitcast_fusion = f32[1,87,8,128]{3,2,1,0:T(8,128)} fusion(f32[88,8,128]{2,1,0:T(8,128)} %get-tuple-element.4), kind=kLoop, calls=%fused_computation | loop fusion | bytes 712704 | tf_op jit(solution)/shard_map/broadcast_in_dim | solution.py:334

commit v5 on v4

v5 whole, which is shorter than its diff:
```python
import functools

import jax
import jax.numpy as jnp
import numpy as np
from jax import lax
from jax.experimental import pallas as pl
from jax.experimental.pallas import tpu as pltpu
from jax.sharding import PartitionSpec as P

LEVELS = 7
SMOOTH_EPS = 0.05
CELL = 8
MESH = pl.DeviceIdType.MESH


def lat_tables(row_count):
    row_index = np.arange(row_count, dtype=np.float32)
    angle = (np.float32(89.875) - np.float32(0.25) * row_index) * np.float32(np.pi / 180.0)
    current = np.cos(angle).astype(np.float32)
    boxes = [current]
    for level in range(LEVELS):
        reach = 2**level
        current = current + np.pad(current, (0, reach))[reach : reach + row_count]
        boxes.append(current)
    return boxes


def box_matrix(shape, cell, anchor, reach):
    source = lax.broadcasted_iota(jnp.int32, shape, cell)
    start = lax.broadcasted_iota(jnp.int32, shape, anchor)
    inside = jnp.where(source >= start, 1.0, 0.0) * jnp.where(source < start + reach, 1.0, 0.0)
    return inside.astype(jnp.bfloat16)


def split(value, count):
    pieces = []
    for _ in range(count):
        piece = value.astype(jnp.bfloat16)
        pieces.append(piece)
        value = value - piece.astype(jnp.float32)
    return jnp.concatenate(pieces, axis=1)


def rows_ahead(tiles, scale):
    count = len(tiles)
    if 2**scale >= count:
        tiles = list(tiles)
        for r in reversed(range(count - 1)):
            tiles[r] = tiles[r] + tiles[r + 1]
        return tiles
    for level in range(scale):
        reach = 2**level
        tiles = [t + tiles[r + reach] if r + reach < count else t for r, t in enumerate(tiles)]
    return tiles


def rows_behind(tiles, scale):
    return rows_ahead(tiles[::-1], scale)[::-1]


def absolute(value):
    square = value * value + SMOOTH_EPS * SMOOTH_EPS
    root = lax.rsqrt(square)
    return square * root, value * root


def kernel(
    sizes, factors, inverses, weights, lat_weight, members_ref, target_ref, grad_ref, loss_ref,
    mem_v, tgt_v, tab_v, ahead_v, behind_v, lhs, boxes, slopes, flat_slope, adjoint,
    sent, field, east, own_adj, east_adj, west_adj, final,
    total, group_loss, lon_loss,
    in_sem, x_send, x_recv, h_send, h_recv, b_send, b_recv, o_send, o_recv, o_own,
    lg_send, lg_recv, ll_send, ll_recv,
):
    channels, rows, cols, bands, sectors, spans = sizes
    group = 2 * bands
    quota = sum(spans)
    chunks = len(spans)
    nlat = rows * bands
    scales = LEVELS + 1
    mem, lat, lon = lax.axis_index("mem"), lax.axis_index("lat"), lax.axis_index("lon")
    me = mem * bands + lat

    def part(k):
        return pl.ds(k * CELL * rows, spans[k] * rows)

    def peer(offset):
        index = lax.rem(me + offset, group)
        return index, {"mem": index // bands, "lat": lax.rem(index, bands), "lon": lon}

    def sector(offset):
        return {"mem": mem, "lat": lat, "lon": lax.rem(lon + offset, sectors)}

    loads = [
        pltpu.make_async_copy(members_ref.at[0], mem_v, in_sem.at[0]),
        pltpu.make_async_copy(target_ref, tgt_v, in_sem.at[1]),
    ]
    for load in loads:
        load.start()
    barrier = pltpu.get_barrier_semaphore()
    for offset in range(1, group):
        pl.semaphore_signal(barrier, inc=1, device_id=peer(offset)[1], device_id_type=MESH)
    for offset in range(1, sectors):
        pl.semaphore_signal(barrier, inc=1, device_id=sector(offset), device_id_type=MESH)

    sub = lax.broadcasted_iota(jnp.int32, (rows, cols), 0)
    zero = jnp.zeros((rows, cols), jnp.float32)
    for band in range(bands):
        tile = jnp.full((rows, cols), lat_weight[band * rows], jnp.float32)
        for r in range(1, rows):
            tile = jnp.where(sub == r, lat_weight[band * rows + r], tile)
        tab_v[band] = tile
    for load in loads:
        load.wait()
    own_weight = tab_v[lat]

    def remote(source, target, send, recv, device):
        return pltpu.make_async_remote_copy(
            src_ref=source, dst_ref=target, send_sem=send, recv_sem=recv,
            device_id=device, device_id_type=MESH,
        )

    def exchange(k, offset):
        index, device = peer(offset)
        return remote(sent.at[index, part(k)], field.at[me, part(k)], x_send.at[k, offset], x_recv.at[k, offset], device)

    def halo(k):
        return remote(field.at[:, part(k)], east.at[:, part(k)], h_send.at[k], h_recv.at[k], sector(sectors - 1))

    def back(k):
        return remote(east_adj.at[:, part(k)], west_adj.at[:, part(k)], b_send.at[k], b_recv.at[k], sector(1))

    def place(k):
        return grad_ref.at[pl.ds((me * quota + k * CELL) * rows, spans[k] * rows)]

    def result(k, offset):
        index, device = peer(offset)
        return remote(final.at[index, part(k)], place(k), o_send.at[k, offset], o_recv.at[k, offset], device)

    def stay(k):
        return pltpu.make_async_copy(final.at[me, part(k)], place(k), o_own.at[k])

    for k in range(chunks):
        for g in range(group):
            base = g * quota + k * CELL
            valid = min(max(channels - base, 0), spans[k])
            start, edge, stop = k * CELL, k * CELL + valid, k * CELL + spans[k]
            if valid > 0:
                difference = mem_v[base : base + valid] - tgt_v[base : base + valid]
                sent[g, start * rows : edge * rows] = (difference * own_weight).reshape(valid * rows, cols)
            if edge < stop:
                sent[g, edge * rows : stop * rows] = jnp.zeros(((stop - edge) * rows, cols), jnp.float32)
        if k == 0:
            pl.semaphore_wait(barrier, group + sectors - 2)
        for offset in range(1, group):
            exchange(k, offset).start()
        field[me, part(k)] = sent[me, part(k)]

    for scale in range(1, scales):
        at = pl.ds((scale - 1) * cols, cols)
        matrix = box_matrix((2 * cols, cols), 0, 1, 2**scale)
        for piece in range(3):
            ahead_v[pl.ds(piece * 2 * cols, 2 * cols), at] = matrix
        matrix = box_matrix((cols, 2 * cols), 1, 0, 2**scale)
        for piece in range(2):
            behind_v[pl.ds((piece * LEVELS + scale - 1) * cols, cols), :] = matrix
    spare = chunks * CELL - quota
    if spare > 0:
        for buffer in (field, east):
            buffer[:, quota * rows : chunks * CELL * rows] = jnp.zeros((group, spare * rows, cols), jnp.float32)

    for k in range(chunks):
        for offset in range(1, group):
            exchange(k, offset).wait_recv()
        halo(k).start()

    total[...] = zero

    def strided(k, r):
        return pl.ds(k * CELL * rows + r, CELL, stride=rows)

    def tile(m, row):
        return pl.ds((m * nlat + row) * CELL, CELL)

    def work(k):
        for m in range(2):
            for row in range(nlat):
                band, r = divmod(row, rows)
                lhs[tile(m, row), 0:cols] = field[m * bands + band, strided(k, r), :]
                lhs[tile(m, row), cols : 2 * cols] = east[m * bands + band, strided(k, r), :]
        boxes[...] = jnp.dot(split(lhs[...], 3), ahead_v[...], preferred_element_type=jnp.float32)
        score = jnp.zeros((CELL, cols), jnp.float32)
        for scale in range(scales):
            at = pl.ds((scale - 1) * cols, cols)
            fields = []
            for m in range(2):
                if scale == 0:
                    fields.append([lhs[tile(m, row), 0:cols] for row in range(nlat)])
                else:
                    fields.append(rows_ahead([boxes[tile(m, row), at] for row in range(nlat)], scale))
            slope = [[], []]
            for row in range(nlat):
                leader = fields[0][row] * inverses[scale][row]
                partner = fields[1][row] * inverses[scale][row]
                first_abs, first_slope = absolute(leader)
                second_abs, second_slope = absolute(partner)
                spread_abs, spread_slope = absolute(leader - partner)
                score = score + weights[scale][row] * (first_abs + second_abs - spread_abs)
                slope[0].append((first_slope - spread_slope) * factors[scale])
                slope[1].append((second_slope + spread_slope) * factors[scale])
            for m in range(2):
                if scale == 0:
                    for row in range(nlat):
                        flat_slope[tile(m, row), :] = slope[m][row]
                else:
                    for row, value in enumerate(rows_behind(slope[m], scale)):
                        slopes[tile(m, row), at] = value
        adjoint[...] = jnp.dot(split(slopes[...], 2), behind_v[...], preferred_element_type=jnp.float32)
        for m in range(2):
            for row in range(nlat):
                band, r = divmod(row, rows)
                own_adj[m * bands + band, strided(k, r), :] = adjoint[tile(m, row), 0:cols] + flat_slope[tile(m, row), :]
                east_adj[m * bands + band, strided(k, r), :] = adjoint[tile(m, row), cols : 2 * cols]
        place_in = k * CELL + lax.broadcasted_iota(jnp.int32, (CELL, cols), 0)
        inside = jnp.where(place_in < quota, 1.0, 0.0) * jnp.where(me * quota + place_in < channels, 1.0, 0.0)
        total[...] += score * inside

    def finish(k):
        back(k).wait_recv()
        for g in range(group):
            summed = (own_adj[g, part(k)] + west_adj[g, part(k)]).reshape(spans[k], rows, cols)
            final[g, part(k)] = (summed * tab_v[g % bands]).reshape(spans[k] * rows, cols)
        for offset in range(1, group):
            result(k, offset).start()
        stay(k).start()

    for k in range(chunks):
        halo(k).wait_recv()
        work(k)
        back(k).start()
        if k > 0:
            finish(k - 1)

    group_loss[me] = total[...]
    group_copies = []
    for offset in range(1, group):
        copy = remote(total, group_loss.at[me], lg_send.at[offset], lg_recv.at[offset], peer(offset)[1])
        copy.start()
        group_copies.append(copy)
    finish(chunks - 1)
    for copy in group_copies:
        copy.wait()
    subtotal = group_loss[0]
    for g in range(1, group):
        subtotal = subtotal + group_loss[g]
    lon_loss[lon] = subtotal
    total[...] = subtotal
    lon_copies = []
    for offset in range(1, sectors):
        copy = remote(total, lon_loss.at[lon], ll_send.at[offset], ll_recv.at[offset], sector(offset))
        copy.start()
        lon_copies.append(copy)
    for copy in lon_copies:
        copy.wait()
    subtotal = lon_loss[0]
    for j in range(1, sectors):
        subtotal = subtotal + lon_loss[j]
    loss_ref[0, 0] = jnp.sum(subtotal)

    for k in range(chunks):
        halo(k).wait_send()
        back(k).wait_send()
        stay(k).wait()
        for offset in range(1, group):
            exchange(k, offset).wait_send()
            result(k, offset).wait()


def shards(members, target):
    channels, rows, cols = target.shape
    bands, sectors = lax.axis_size("lat"), lax.axis_size("lon")
    assert lax.axis_size("mem") == 2 and cols >= 2**LEVELS
    group = 2 * bands
    quota = -(-channels // group)
    chunks = -(-quota // CELL)
    spans = [min(CELL, quota - k * CELL) for k in range(chunks)]
    scales = LEVELS + 1
    nlat, nlon = rows * bands, cols * sectors

    boxes = lat_tables(nlat)
    sums = [float(np.sum(box.astype(np.float64))) for box in boxes]
    inverses = [(1.0 / (2.0**s * boxes[s].astype(np.float64))).tolist() for s in range(scales)]
    weights = [(0.5 * boxes[s].astype(np.float64) / (channels * nlon * sums[s])).tolist() for s in range(scales)]
    factors = [0.5 * nlat / (sums[s] * 2.0**s) for s in range(scales)]

    sizes = (channels, rows, cols, bands, sectors, spans)
    blocks = pltpu.VMEM((group, chunks * CELL * rows, cols), jnp.float32)
    lines = 2 * nlat * CELL
    dma = pltpu.SemaphoreType.DMA
    gradient, loss = pl.pallas_call(
        functools.partial(kernel, sizes, factors, inverses, weights, boxes[0].tolist()),
        out_shape=(
            jax.ShapeDtypeStruct((group * quota * rows, cols), jnp.float32),
            jax.ShapeDtypeStruct((1, 1), jnp.float32),
        ),
        in_specs=[pl.BlockSpec(memory_space=pl.ANY)] * 2,
        out_specs=(pl.BlockSpec(memory_space=pl.ANY), pl.BlockSpec(memory_space=pltpu.SMEM)),
        scratch_shapes=[
            pltpu.VMEM((channels, rows, cols), jnp.float32),
            pltpu.VMEM((channels, rows, cols), jnp.float32),
            pltpu.VMEM((bands, rows, cols), jnp.float32),
            pltpu.VMEM((6 * cols, LEVELS * cols), jnp.bfloat16),
            pltpu.VMEM((2 * LEVELS * cols, 2 * cols), jnp.bfloat16),
            pltpu.VMEM((lines, 2 * cols), jnp.float32),
            pltpu.VMEM((lines, LEVELS * cols), jnp.float32),
            pltpu.VMEM((lines, LEVELS * cols), jnp.float32),
            pltpu.VMEM((lines, cols), jnp.float32),
            pltpu.VMEM((lines, 2 * cols), jnp.float32),
            blocks, blocks, blocks, blocks, blocks, blocks, blocks,
            pltpu.VMEM((rows, cols), jnp.float32),
            pltpu.VMEM((group, rows, cols), jnp.float32),
            pltpu.VMEM((sectors, rows, cols), jnp.float32),
            dma((2,)),
            dma((chunks, group)), dma((chunks, group)),
            dma((chunks,)), dma((chunks,)),
            dma((chunks,)), dma((chunks,)),
            dma((chunks, group)), dma((chunks, group)), dma((chunks,)),
            dma((group,)), dma((group,)),
            dma((sectors,)), dma((sectors,)),
        ],
        compiler_params=pltpu.CompilerParams(
            collective_id=0, has_side_effects=True, vmem_limit_bytes=60 * 1024 * 1024
        ),
    )(members, target)
    return gradient.reshape(1, group * quota, rows, cols)[:, :channels], loss[0, 0]


def solution(mesh):
    return jax.shard_map(
        shards,
        mesh=mesh,
        in_specs=(P("mem", None, "lat", "lon"), P(None, "lat", "lon")),
        out_specs=(P("mem", None, "lat", "lon"), P()),
        check_vma=False,
    )
```

time: 33.5 us -> 33.2 us (level)
    broadcast_in_dim x1 -> x0, local copies, waits for them, and re-layouts: 1.74 us -> none  [shards(): return (gradient[None, :channels], loss[0, 0])]
    slice x0 -> x1, local copies, waits for them, and re-layouts: none -> 1.74 us  [shards(): gradient.reshape(1, group * quota, rows, cols)[:, :channels]]
where the time goes in v5:
time: 33.2 us; the launch traced here: 33 us
  Pallas kernels  28.9 us (87%)
  between operations  2.4 us (7%)
  local copies, waits for them, and re-layouts  1.74 us (5%)
    pallas_call x1, Pallas kernels, shards(): pl.pallas_call(functools.partial(kernel, sizes, factors, inverses, weight...  28.9 us
    slice x1, local copies, waits for them, and re-layouts, shards(): gradient.reshape(1, group * quota, rows, cols)[:, :channels]  1.74 us

profile of v5, /device:TPU:0, one launch (start us, length us, event | category | flops | bytes accessed | tf_op | source)
XLA Modules:
  0.0 33.0 jit_solution(15455720552250364907)
XLA Ops:
  0.6 28.9 %shard_map.41 = (f32[704,128]{1,0:T(8,128)}, f32[1,1]{1,0:T(1,128)}) custom-call(f32[1,87,8,128]{3,2,1,0:T(8,128)} %members_ref.1, f32[87,8,128]{2,1,0:T(8,128)} %target_ref.1), custom_call_target="tpu_custom_call" | custom-call | tf_op jit(solution)/shard_map/pallas_call | solution.py:301
  29.5 1.7 %slice.4 = f32[1,87,8,128]{3,2,1,0:T(8,128)} slice(f32[1,88,8,128]{3,2,1,0:T(8,128)} %bitcast.2), slice={[0:1], [0:87], [0:8], [0:128]} | slice | bytes 712704 | tf_op jit(solution)/shard_map/slice | solution.py:336

commit v6 on v5

--- a/solution.py
+++ b/solution.py
@@ -153,8 +153,8 @@
                 sent[g, edge * rows : stop * rows] = jnp.zeros(((stop - edge) * rows, cols), jnp.float32)
         if k == 0:
             pl.semaphore_wait(barrier, group + sectors - 2)
-        for offset in range(1, group):
-            exchange(k, offset).start()
+            for offset in range(1, group):
+                exchange(k, offset).start()
         field[me, part(k)] = sent[me, part(k)]
 
     for scale in range(1, scales):
@@ -173,6 +173,9 @@
     for k in range(chunks):
         for offset in range(1, group):
             exchange(k, offset).wait_recv()
+        if k + 1 < chunks:
+            for offset in range(1, group):
+                exchange(k + 1, offset).start()
         halo(k).start()
 
     total[...] = zero
@@ -239,16 +242,16 @@
         halo(k).wait_recv()
         work(k)
         back(k).start()
+        if k + 1 == chunks:
+            group_loss[me] = total[...]
+            group_copies = []
+            for offset in range(1, group):
+                copy = remote(total, group_loss.at[me], lg_send.at[offset], lg_recv.at[offset], peer(offset)[1])
+                copy.start()
+                group_copies.append(copy)
         if k > 0:
             finish(k - 1)
 
-    group_loss[me] = total[...]
-    group_copies = []
-    for offset in range(1, group):
-        copy = remote(total, group_loss.at[me], lg_send.at[offset], lg_recv.at[offset], peer(offset)[1])
-        copy.start()
-        group_copies.append(copy)
-    finish(chunks - 1)
     for copy in group_copies:
         copy.wait()
     subtotal = group_loss[0]
@@ -261,6 +264,7 @@
         copy = remote(total, lon_loss.at[lon], ll_send.at[offset], ll_recv.at[offset], sector(offset))
         copy.start()
         lon_copies.append(copy)
+    finish(chunks - 1)
     for copy in lon_copies:
         copy.wait()
     subtotal = lon_loss[0]

time: 33.2 us -> 35.7 us (1.075)
  Pallas kernels: 28.9 us -> 31.4 us
    pallas_call x1, Pallas kernels: 28.9 us -> 31.4 us  [shards(): pl.pallas_call(functools.partial(kernel, sizes, factors, inverses, weight...]
where the time goes in v6:
time: 35.7 us; the launch traced here: 35.5 us
  Pallas kernels  31.4 us (88%)
  between operations  2.4 us (7%)
  local copies, waits for them, and re-layouts  1.74 us (5%)
    pallas_call x1, Pallas kernels, shards(): pl.pallas_call(functools.partial(kernel, sizes, factors, inverses, weight...  31.4 us
    slice x1, local copies, waits for them, and re-layouts, shards(): gradient.reshape(1, group * quota, rows, cols)[:, :channels]  1.74 us

profile of v6, /device:TPU:0, one launch (start us, length us, event | category | flops | bytes accessed | tf_op | source)
XLA Modules:
  0.0 35.5 jit_solution(2342124204806727268)
XLA Ops:
  0.6 31.4 %shard_map.41 = (f32[704,128]{1,0:T(8,128)}, f32[1,1]{1,0:T(1,128)}) custom-call(f32[1,87,8,128]{3,2,1,0:T(8,128)} %members_ref.1, f32[87,8,128]{2,1,0:T(8,128)} %target_ref.1), custom_call_target="tpu_custom_call" | custom-call | tf_op jit(solution)/shard_map/pallas_call | solution.py:305
  32.0 1.7 %slice.4 = f32[1,87,8,128]{3,2,1,0:T(8,128)} slice(f32[1,88,8,128]{3,2,1,0:T(8,128)} %bitcast.2), slice={[0:1], [0:87], [0:8], [0:128]} | slice | bytes 712704 | tf_op jit(solution)/shard_map/slice | solution.py:340

commit v7 on v6

--- a/solution.py
+++ b/solution.py
@@ -125,8 +125,12 @@
         index, device = peer(offset)
         return remote(sent.at[index, part(k)], field.at[me, part(k)], x_send.at[k, offset], x_recv.at[k, offset], device)
 
-    def halo(k):
-        return remote(field.at[:, part(k)], east.at[:, part(k)], h_send.at[k], h_recv.at[k], sector(sectors - 1))
+    def halo(k, offset):
+        index = lax.rem(me + group - offset, group)
+        return remote(
+            field.at[index, part(k)], east.at[index, part(k)], h_send.at[k, offset], h_recv.at[k, offset],
+            sector(sectors - 1),
+        )
 
     def back(k):
         return remote(east_adj.at[:, part(k)], west_adj.at[:, part(k)], b_send.at[k], b_recv.at[k], sector(1))
@@ -153,9 +157,10 @@
                 sent[g, edge * rows : stop * rows] = jnp.zeros(((stop - edge) * rows, cols), jnp.float32)
         if k == 0:
             pl.semaphore_wait(barrier, group + sectors - 2)
-            for offset in range(1, group):
-                exchange(k, offset).start()
+        for offset in range(1, group):
+            exchange(k, offset).start()
         field[me, part(k)] = sent[me, part(k)]
+        halo(k, 0).start()
 
     for scale in range(1, scales):
         at = pl.ds((scale - 1) * cols, cols)
@@ -171,12 +176,9 @@
             buffer[:, quota * rows : chunks * CELL * rows] = jnp.zeros((group, spare * rows, cols), jnp.float32)
 
     for k in range(chunks):
-        for offset in range(1, group):
+        for offset in [group // 2] + [o for o in range(1, group) if o != group // 2]:
             exchange(k, offset).wait_recv()
-        if k + 1 < chunks:
-            for offset in range(1, group):
-                exchange(k + 1, offset).start()
-        halo(k).start()
+            halo(k, offset).start()
 
     total[...] = zero
 
@@ -239,7 +241,8 @@
         stay(k).start()
 
     for k in range(chunks):
-        halo(k).wait_recv()
+        for offset in range(group):
+            halo(k, offset).wait_recv()
         work(k)
         back(k).start()
         if k + 1 == chunks:
@@ -273,7 +276,8 @@
     loss_ref[0, 0] = jnp.sum(subtotal)
 
     for k in range(chunks):
-        halo(k).wait_send()
+        for offset in range(group):
+            halo(k, offset).wait_send()
         back(k).wait_send()
         stay(k).wait()
         for offset in range(1, group):
@@ -327,7 +331,7 @@
             pltpu.VMEM((sectors, rows, cols), jnp.float32),
             dma((2,)),
             dma((chunks, group)), dma((chunks, group)),
-            dma((chunks,)), dma((chunks,)),
+            dma((chunks, group)), dma((chunks, group)),
             dma((chunks,)), dma((chunks,)),
             dma((chunks, group)), dma((chunks, group)), dma((chunks,)),
             dma((group,)), dma((group,)),

time: 35.7 us -> 33.2 us (0.930)
  Pallas kernels: 31.4 us -> 28.8 us
    pallas_call x1, Pallas kernels: 31.4 us -> 28.8 us  [shards(): pl.pallas_call(functools.partial(kernel, sizes, factors, inverses, weight...]
where the time goes in v7:
time: 33.2 us; the launch traced here: 33 us
  Pallas kernels  28.8 us (87%)
  between operations  2.4 us (7%)
  local copies, waits for them, and re-layouts  1.74 us (5%)
    pallas_call x1, Pallas kernels, shards(): pl.pallas_call(functools.partial(kernel, sizes, factors, inverses, weight...  28.8 us
    slice x1, local copies, waits for them, and re-layouts, shards(): gradient.reshape(1, group * quota, rows, cols)[:, :channels]  1.74 us

profile of v7, /device:TPU:0, one launch (start us, length us, event | category | flops | bytes accessed | tf_op | source)
XLA Modules:
  0.0 33.0 jit_solution(10784125915121313330)
XLA Ops:
  0.6 28.8 %shard_map.41 = (f32[704,128]{1,0:T(8,128)}, f32[1,1]{1,0:T(1,128)}) custom-call(f32[1,87,8,128]{3,2,1,0:T(8,128)} %members_ref.1, f32[87,8,128]{2,1,0:T(8,128)} %target_ref.1), custom_call_target="tpu_custom_call" | custom-call | tf_op jit(solution)/shard_map/pallas_call | solution.py:309
  29.5 1.7 %slice.4 = f32[1,87,8,128]{3,2,1,0:T(8,128)} slice(f32[1,88,8,128]{3,2,1,0:T(8,128)} %bitcast.2), slice={[0:1], [0:87], [0:8], [0:128]} | slice | bytes 712704 | tf_op jit(solution)/shard_map/slice | solution.py:344
